TPU v7x, 512 devices: a whole 4x8x8 slice. The times are simulated.
512 devices in a mesh: dp: 64 (over z, y), tile: 8 (over x, core).
Axes of the slice: x: 4, y: 8, z: 8, core: 2. Of those that a mesh axis runs over, the one named last changes fastest.
Arguments:
- embeddings: bfloat16 [262144, 768], P('dp'), may hold values from -30 to 30
- cluster_ids: int32 [262144], P('dp'), may hold values from 0 to 255, as said below
- padding: int32 [262144], P('dp'), may hold values from 0 to 1
Outputs:
- nearest: float32 [262144], P('dp')
Inputs may be any that keep to these rules, and one draw needn't show every extreme that they name: cluster_ids is used only where padding is 0. Among the unpadded rows of one dp index (aligned blocks of 4096 rows), at most 64 have cluster ids of one residue modulo 64. In every draw some block has exactly 64 unpadded rows of every residue, and some residue takes exactly 64 rows from every block.
All inputs are finite; a program needn't handle non-finite values.
Results may differ from a plain program's by a relative error of at most 0.0003.
Values may be sent and summed in bfloat16 or wider, within the bound.
No kernel may reach another device: no remote copies, remote signals or barrier semaphores. Data moves between devices by JAX's collectives and lax.ppermute only.
A program may use at most 64 MiB of HBM per device.

v0:
```python
import jax
import jax.numpy as jnp
from jax import lax
from jax.sharding import PartitionSpec as P


def on_device(embeddings, cluster_ids, padding):
    owner_count = lax.axis_size("dp")
    tile_count = lax.axis_size("tile")
    row_count, feature_count = embeddings.shape
    capacity = row_count // owner_count
    col_block = capacity // tile_count
    col_start = lax.axis_index("tile") * col_block
    values = embeddings.astype(jnp.float32)
    unit = (values * lax.rsqrt(jnp.sum(values * values, axis=1, keepdims=True) + 1e-06)).astype(
        jnp.bfloat16
    )
    unpadded = padding == 0
    owner_of = cluster_ids % owner_count
    member = (
        (owner_of[:, None] == jnp.arange(owner_count, dtype=jnp.int32)[None, :]) & unpadded[:, None]
    ).astype(jnp.int32)
    earlier = jnp.cumsum(member, axis=0) - member
    slot_of = jnp.sum(earlier * member, axis=1)
    target = jnp.where(unpadded, owner_of * capacity + slot_of, owner_count * capacity)
    outgoing = (
        jnp.zeros((owner_count * capacity, feature_count), jnp.bfloat16)
        .at[target]
        .set(unit, mode="drop")
    )
    outgoing = outgoing.reshape(owner_count, capacity, feature_count)
    outgoing_ids = (
        jnp.full((owner_count * capacity,), -1, jnp.int32).at[target].set(cluster_ids, mode="drop")
    )
    outgoing_ids = outgoing_ids.reshape(owner_count, capacity)
    got_ids = lax.all_to_all(outgoing_ids, "dp", split_axis=0, concat_axis=0, tiled=True)
    col_ids = lax.dynamic_slice_in_dim(got_ids, col_start, col_block, 1).reshape(-1)
    col_source = lax.broadcasted_iota(jnp.int32, (owner_count, col_block), 0).reshape(-1)
    col_slot = (col_start + lax.broadcasted_iota(jnp.int32, (owner_count, col_block), 1)).reshape(
        -1
    )
    received = lax.all_to_all(outgoing, "dp", split_axis=0, concat_axis=0, tiled=True)
    columns = lax.dynamic_slice_in_dim(received, col_start, col_block, 1).reshape(-1, feature_count)
    piece_width = received.shape[1]
    rows_flat = received.reshape(-1, feature_count)
    scores = lax.dot_general(
        rows_flat, columns, (((1,), (1,)), ((), ())), preferred_element_type=jnp.float32
    )
    row_ids = got_ids.reshape(-1)
    row_source = lax.broadcasted_iota(jnp.int32, (owner_count, piece_width), 0).reshape(-1)
    row_slot = lax.broadcasted_iota(jnp.int32, (owner_count, piece_width), 1).reshape(-1)
    itself = (row_source[:, None] == col_source[None, :]) & (row_slot[:, None] == col_slot[None, :])
    allowed = (
        (row_ids[:, None] == col_ids[None, :]) & (col_ids[None, :] >= 0) & jnp.logical_not(itself)
    )
    partial_value = jnp.max(jnp.where(allowed, scores, jnp.float32(-1.0)), axis=1).reshape(
        owner_count, piece_width
    )
    sendback = lax.pmax(partial_value, "tile")
    returned = lax.all_to_all(sendback, "dp", split_axis=0, concat_axis=0, tiled=True).reshape(-1)
    picked = jnp.take(returned, jnp.minimum(target, owner_count * capacity - 1), axis=0)
    nearest = jnp.where(unpadded, picked, jnp.float32(-1.0))
    return nearest


def solution(mesh):
    in_specs = (P("dp", None), P("dp"), P("dp"))
    out_specs = P("dp")
    return jax.shard_map(
        on_device, mesh=mesh, in_specs=in_specs, out_specs=out_specs, check_vma=False
    )
```

profile of v0, /device:TPU:1, one launch (start us, length us, event | category | flops | bytes accessed | tf_op | source)
XLA Modules:
  0.0 372.7 jit_solution(7072165473009496589)
XLA Ops:
  0.0 0.8 fusion.21
  0.8 0.7 broadcast_compare_fusion
  1.5 0.7 add_select_fusion
  2.4 18.4 %reduce-window.6 = s32[64,32,128]{2,1,0:T(8,128)S(1)} reduce-window(s32[64,32,128]{2,1,0:T(8,128)S(1)} %fusion.11, s32[]{:T(128)} %constant.19.clone.1), window={size=1x1x128 pad=0_0x0_0x127_0}, to_apply=%region_0.0 | reduce-window | flops 33292288 | bytes 2097156 | tf_op jit(solution)/shard_map/reduce-window
  20.8 0.3 slice.10
  21.2 0.4 copy.8
  21.8 0.3 broadcast_add_fusion
  22.2 0.9 fusion.8
  23.1 15.5 %scatter_custom_fusion = s32[4096]{0:T(1024)S(1)} fusion(s32[4096]{0:T(1024)S(1)} %compare_select_fusion, s32[4096]{0:T(1024)S(1)} %copy-done.1, s32[]{:T(128)} %constant.28.clone.1), kind=kCustom, calls=%fused_computation.34 | custom fusion | bytes 16388 | tf_op jit(solution)/shard_map/scatter | solution.py:33
  38.7 0.7 all_to_all.15
  39.4 17.1 %all-to-all-start = ((s32[64,1,64]{2,1,0:T(1,128)}), s32[64,1,64]{2,1,0:T(1,128)S(1)}, u32[]{:S(2)}, u32[]{:S(2)}) async-start(s32[64,1,64]{2,1,0:T(1,128)} %all_to_all.15), calls=%async_computation | async-start | bytes 65536 | tf_op jit(solution)/shard_map/all_to_all | solution.py:36
  56.5 4.1 %fusion = f32[4096]{0:T(1024)S(1)} fusion(bf16[4096,768]{1,0:T(8,128)(2,1)} %param.3), kind=kLoop, calls=%fused_computation.5 | loop fusion | flops 9433088 | bytes 6307840 | tf_op jit(solution)/shard_map/reduce_sum | solution.py:15
  60.6 24.1 %scatter_custom_fusion.1 = bf16[4096,768]{1,0:T(8,128)(2,1)} fusion(s32[4096]{0:T(1024)S(1)} %compare_select_fusion, bf16[4096,768]{1,0:T(8,128)(2,1)} %param.3, f32[4096]{0:T(1024)S(1)} %add_rsqrt_fusion, bf16[]{:T(256)} %constant.54.clone.1), kind=kCustom, calls=%fused_computation.8 | custom fusion | flops 9437184 | bytes 12599298 | tf_op jit(solution)/shard_map/scatter | solution.py:29
  84.7 12.4 %all-to-all-start.1 = ((bf16[64,64,768]{2,1,0:T(8,128)(2,1)}), bf16[64,64,768]{2,1,0:T(8,128)(2,1)}, u32[]{:S(2)}, u32[]{:S(2)}) async-start(bf16[64,64,768]{2,1,0:T(8,128)(2,1)} %bitcast.30), calls=%async_computation.1 | async-start | bytes 12582912 | tf_op jit(solution)/shard_map/all_to_all | solution.py:42
  97.5 0.5 broadcast.68
  98.0 0.7 reduce.10
  99.1 182.7 %all-to-all-done.1 = bf16[64,64,768]{2,1,0:T(8,128)(2,1)} async-done(((bf16[64,64,768]{2,1,0:T(8,128)(2,1)}), bf16[64,64,768]{2,1,0:T(8,128)(2,1)}, u32[]{:S(2)}, u32[]{:S(2)}) %all-to-all-start.1) | async-done | bytes 6291488 | tf_op jit(solution)/shard_map/all_to_all | solution.py:42
  281.8 7.1 %select_reduce_fusion = f32[4096]{0:T(1024)S(1)} fusion(bf16[4096,768]{1,0:T(8,128)(2,1)} %bitcast.6, s32[4096]{0:T(1024)S(1)} %eq.97, s32[4096]{0:T(1024)S(1)} %eq.92, s32[4096]{0:T(1024)S(1)} %eq.87, s32[512]{0:T(512)S(1)} %eq.99, s32[512]{0:T(512)S(1)} %eq.94, s32[512]{0:T(512)S(1)} %eq.89, pred[512]{0:T(512)(128)(4,1)S(1)} %broadcast_compare_fusion.1, ...), kind=kOutput, calls=%fused_computation.7 | convolution fusion | flops 3240095744 | bytes 7150084 | tf_op jit(solution)/shard_map/dot_general | solution.py:46
  289.0 24.8 %pmax.7 = f32[64,1,64]{2,1,0:T(1,128)S(1)} all-reduce(f32[64,1,64]{2,1,0:T(1,128)S(1)} %all_to_all.18), channel_id=1, replica_groups=mesh['dp'=64,'tile'=8] {'tile'}, use_global_device_ids=true, to_apply=%region_7.8 | all-reduce | flops 4096 | bytes 32768 | tf_op jit(solution)/shard_map/pmax | solution.py:59
  313.7 34.0 %all_to_all.23 = f32[64,1,64]{2,1,0:T(1,128)S(1)} all-to-all(f32[64,1,64]{2,1,0:T(1,128)S(1)} %pmax.7), channel_id=1, replica_groups=mesh['dp'=64,'tile'=8] {'dp'}, dimensions={0} | all-to-all | bytes 32768 | tf_op jit(solution)/shard_map/all_to_all | solution.py:60
  347.7 0.5 broadcast.69
  348.2 0.7 reduce.11
  349.0 23.0 %gather_fusion = f32[4096]{0:T(1024)S(1)} fusion(f32[4096]{0:T(1024)S(1)} %reshape.76, s32[4096]{0:T(1024)S(1)} %get-tuple-element.5), kind=kCustom, calls=%fused_computation | custom fusion | bytes 49152 | tf_op jit(solution)/shard_map/jit(_take)/gather | solution.py:61
  372.1 0.6 select_select_fusion
  (25 shorter events, 1.2 us)
Async XLA Ops:
  0.0 23.1 %copy-start = (s32[4096]{0:T(1024)S(1)}, s32[4096]{0:T(1024)}, u32[]{:S(2)}) copy-start(s32[4096]{0:T(1024)} %param.5) | copy-start | bytes 49156
  0.0 23.1 %copy-start.1 = (s32[4096]{0:T(1024)S(1)}, s32[4096]{0:T(1024)}, u32[]{:S(2)}) copy-start(s32[4096]{0:T(1024)} %param.4) | copy-start | bytes 49156
  39.4 45.4 %all-to-all-start = ((s32[64,1,64]{2,1,0:T(1,128)}), s32[64,1,64]{2,1,0:T(1,128)S(1)}, u32[]{:S(2)}, u32[]{:S(2)}) async-start(s32[64,1,64]{2,1,0:T(1,128)} %all_to_all.15), calls=%async_computation | async-start | bytes 65536 | tf_op jit(solution)/shard_map/all_to_all | solution.py:36
  84.7 197.1 %all-to-all-start.1 = ((bf16[64,64,768]{2,1,0:T(8,128)(2,1)}), bf16[64,64,768]{2,1,0:T(8,128)(2,1)}, u32[]{:S(2)}, u32[]{:S(2)}) async-start(bf16[64,64,768]{2,1,0:T(8,128)(2,1)} %bitcast.30), calls=%async_computation.1 | async-start | bytes 12582912 | tf_op jit(solution)/shard_map/all_to_all | solution.py:42
where the time goes:
time: 376 us; the launch traced here: 373 us
  waiting for transfers between devices  183 us (49%)
  blocking collectives  58.7 us (16%)
  other arithmetic  52.6 us (14%)
  local copies, waits for them, and re-layouts  41.9 us (11%)
  starting transfers between devices  29.5 us (8%)
  matrix products  7.09 us (2%)
    all_to_all x1, waiting for transfers between devices, on_device(): lax.all_to_all(outgoing, 'dp', split_axis=0, concat_axis=0, tiled=True)  183 us
    all_to_all x1, blocking collectives, on_device(): lax.all_to_all(sendback, 'dp', split_axis=0, concat_axis=0, tiled=True)  34 us
    pmax x1, blocking collectives, on_device(): sendback = lax.pmax(partial_value, 'tile')  24.8 us
    scatter x1, other arithmetic, on_device(): outgoing = jnp.zeros((owner_count * capacity, feature_count), jnp.bfloat1...  24.1 us
    gather x1, local copies, waits for them, and re-layouts, on_device(): jnp.take(returned, jnp.minimum(target, owner_count * capacity - 1), axis=0)  23 us
    another operation x3, other arithmetic  19 us
    all_to_all x1, starting transfers between devices, on_device(): lax.all_to_all(outgoing_ids, 'dp', split_axis=0, concat_axis=0, tiled=True)  17.1 us
    scatter x1, local copies, waits for them, and re-layouts, on_device(): jnp.full((owner_count * capacity,), -1, jnp.int32).at[target]  15.5 us
  transfers between devices with their start and end apart: 2, of which 1 were waited for; matrix products, arithmetic and copies ran while one was open for 8% of the time, Pallas kernels for 0%

commit v1 on v0

v1 whole, which is shorter than its diff:
```python
import functools

import jax
import jax.numpy as jnp
from jax import lax
from jax.experimental import pallas as pl
from jax.experimental.pallas import tpu as pltpu
from jax.sharding import PartitionSpec as P

OWNERS = 64
CAPACITY = 64
TILES = 8
PART = CAPACITY // TILES
ROWS = OWNERS * PART
TAG = 2.0
VMEM = 60 * 1024 * 1024


def iota(shape, dim):
    return lax.broadcasted_iota(jnp.int32, shape, dim)


def nt_dot(a, b):
    return lax.dot_general(a, b, (((1,), (1,)), ((), ())), preferred_element_type=jnp.float32)


def one_hot(flags):
    return jnp.where(flags, jnp.float32(1), jnp.float32(0)).astype(jnp.bfloat16)


def pack_kernel(tile_ref, ids_ref, padding_ref, emb_ref, unit_ref, place_ref, tags):
    rows = ids_ref.shape[1]
    width = 256
    ids = ids_ref[...]
    owner = jnp.where(padding_ref[...] == 0, ids % OWNERS, -1)
    member = owner == iota((OWNERS, rows), 0)
    member_hot = one_hot(member)
    strictly_before = one_hot(iota((width, width), 0) < iota((width, width), 1))
    carry = jnp.zeros((OWNERS, 1), jnp.float32)
    slots = []
    for start in range(0, rows, width):
        block = member_hot[:, start : start + width]
        rank = carry + jnp.dot(block, strictly_before, preferred_element_type=jnp.float32)
        block = block.astype(jnp.float32)
        slots.append(jnp.sum(block * rank, axis=0, keepdims=True))
        carry = carry + jnp.sum(block, axis=1, keepdims=True)
    slot = jnp.concatenate(slots, axis=1).astype(jnp.int32)
    place_ref[...] = jnp.where(owner >= 0, owner * CAPACITY + slot, -1)
    part = slot // PART
    local = slot % PART
    wanted = jnp.where((owner >= 0) & (part == tile_ref[0]), owner * PART + local, -1)
    total = jnp.zeros((ROWS, emb_ref.shape[1]), jnp.float32)
    step = 1024
    for start in range(0, rows, step):
        pick = one_hot(iota((ROWS, step), 0) == wanted[:, start : start + step])
        total = total + jnp.dot(
            pick, emb_ref[start : start + step, :], preferred_element_type=jnp.float32
        )
    scale = lax.rsqrt(jnp.sum(total * total, axis=1, keepdims=True) + 1e-06)
    features = emb_ref.shape[1]
    unit_ref[:, :features] = (total * scale).astype(jnp.bfloat16)
    marks = TILES * 4
    mark = jnp.where(owner >= 0, local * marks + part * 4 + ids // OWNERS, -1)
    mark_hot = one_hot(iota((PART * marks, rows), 0) == mark)
    by_owner = TAG * nt_dot(member_hot, mark_hot)
    tags[...] = jnp.zeros(tags.shape, jnp.float32)
    for i in range(PART):
        tags[:, i, :marks] = by_owner[:, i * marks : (i + 1) * marks]
    unit_ref[:, features:] = tags[...].reshape(ROWS, 128).astype(jnp.bfloat16)


def marks_of(tag, group):
    lane, mark = iota((128, 128), 0), iota((128, 128), 1)
    take = one_hot((lane == group * 4 + mark) & (mark < 4))
    return jnp.dot(tag, take, preferred_element_type=jnp.float32).astype(jnp.bfloat16)


def spread(best, group):
    row, lane = iota((ROWS, 128), 0), iota((ROWS, 128), 1)
    value = jnp.maximum(best - TAG * TAG, -1.0)
    placed = jnp.where(lane == group * PART + row % PART, value, -2.0)
    return jnp.max(placed.reshape(OWNERS, PART, 128), axis=1)


def own_kernel(groups_ref, tag_ref, a_ref, b_ref, out_ref):
    tag = tag_ref[...]
    marks_a, marks_b = marks_of(tag, groups_ref[0]), marks_of(tag, groups_ref[1])
    a = a_ref[...]
    same = nt_dot(a, a) + nt_dot(marks_a, marks_a)
    same = jnp.where(iota((ROWS, ROWS), 0) == iota((ROWS, ROWS), 1), -2.0, same)
    other = nt_dot(a, b_ref[...]) + nt_dot(marks_a, marks_b)
    best = jnp.max(jnp.maximum(same, other), axis=1, keepdims=True)
    out_ref[...] = spread(best, groups_ref[0])


def cross_kernel(groups_ref, tag_ref, own_ref, a_ref, b_ref, p_ref, n_ref, out_ref):
    tag = tag_ref[...]
    marks_n = marks_of(tag, groups_ref[3])
    columns = n_ref[...]
    out = own_ref[...]
    best_n = jnp.full((8, ROWS), -2.0, jnp.float32)
    for j, ref in enumerate((a_ref, b_ref, p_ref)):
        scores = nt_dot(ref[...], columns) + nt_dot(marks_of(tag, groups_ref[j]), marks_n)
        out = jnp.maximum(out, spread(jnp.max(scores, axis=1, keepdims=True), groups_ref[j]))
        best_n = jnp.maximum(best_n, jnp.max(scores.reshape(ROWS // 8, 8, ROWS), axis=0))
    best_n = jnp.broadcast_to(jnp.max(best_n, axis=0, keepdims=True), (128, ROWS)).T
    out_ref[...] = jnp.maximum(out, spread(best_n[:, :1], groups_ref[3]))


def pick_kernel(place_ref, best_ref, out_ref):
    place = place_ref[...]
    rows = place.shape[1]
    owner_hot = one_hot(place // CAPACITY == iota((OWNERS, rows), 0))
    best = best_ref[...].T
    high = best.astype(jnp.bfloat16)
    rest = best - high.astype(jnp.float32)
    middle = rest.astype(jnp.bfloat16)
    low = (rest - middle.astype(jnp.float32)).astype(jnp.bfloat16)
    by_slot = (
        jnp.dot(high, owner_hot, preferred_element_type=jnp.float32)
        + jnp.dot(middle, owner_hot, preferred_element_type=jnp.float32)
        + jnp.dot(low, owner_hot, preferred_element_type=jnp.float32)
    )
    here = place % CAPACITY == iota((CAPACITY, rows), 0)
    picked = jnp.sum(jnp.where(here, by_slot, 0.0), axis=0, keepdims=True)
    out_ref[...] = jnp.where(place >= 0, picked, -1.0)


def call(kernel, out_shape, in_specs, flops=0, scratch=()):
    return pl.pallas_call(
        kernel,
        out_shape=out_shape,
        in_specs=in_specs,
        scratch_shapes=list(scratch),
        compiler_params=pltpu.CompilerParams(vmem_limit_bytes=VMEM),
        cost_estimate=pl.CostEstimate(flops=flops, bytes_accessed=1 << 20, transcendentals=0),
    )


def on_device(embeddings, cluster_ids, padding):
    rows, features = embeddings.shape
    tile = lax.axis_index("tile")
    chip, core = tile // 2, tile % 2
    vmem = pl.BlockSpec(memory_space=pltpu.VMEM)
    smem = pl.BlockSpec(memory_space=pltpu.SMEM)
    packed, place = call(
        pack_kernel,
        (
            jax.ShapeDtypeStruct((ROWS, features + 128), jnp.bfloat16),
            jax.ShapeDtypeStruct((1, rows), jnp.int32),
        ),
        [smem, vmem, vmem, vmem],
        scratch=[pltpu.VMEM((OWNERS, PART, 128), jnp.float32)],
    )(tile.reshape(1), cluster_ids.reshape(1, rows), padding.reshape(1, rows), embeddings)
    packed = packed.reshape(OWNERS, PART, features + 128)
    received = lax.all_to_all(packed, "dp", split_axis=0, concat_axis=0, tiled=True)
    received = received.reshape(ROWS, features + 128)
    a, tag = received[:, :features], received[:, features:]
    swap = [(2 * x + c, 2 * x + 1 - c) for x in range(4) for c in range(2)]
    forward = [(2 * x + c, 2 * ((x + 1) % 4) + c) for x in range(4) for c in range(2)]
    backward = [
        (2 * ((x + 1) % 4) + (c if x < 2 else 1 - c), 2 * x + c) for x in range(4) for c in range(2)
    ]
    b = lax.ppermute(a, "tile", swap)
    p = lax.ppermute(a, "tile", forward)
    n = lax.ppermute(a, "tile", backward)
    groups = jnp.stack(
        [
            tile,
            2 * chip + 1 - core,
            2 * ((chip + 3) % 4) + core,
            2 * ((chip + 1) % 4) + jnp.where(chip < 2, core, 1 - core),
        ]
    ).astype(jnp.int32)
    partial_shape = jax.ShapeDtypeStruct((OWNERS, 128), jnp.float32)
    own = call(
        own_kernel,
        partial_shape,
        [smem, vmem, vmem, vmem],
        flops=2 * ROWS * 2 * ROWS * features,
    )(groups, tag, a, b)
    best = call(
        cross_kernel,
        partial_shape,
        [smem, vmem, vmem, vmem, vmem, vmem, vmem],
        flops=2 * 3 * ROWS * ROWS * features,
    )(groups, tag, own, a, b, p, n)
    best = best[:, :CAPACITY]
    best = lax.all_to_all(best, "dp", split_axis=0, concat_axis=0, tiled=True)
    best = lax.pmax(best, "tile")
    nearest = call(
        pick_kernel,
        jax.ShapeDtypeStruct((1, rows), jnp.float32),
        [vmem, vmem],
    )(place, best)
    return nearest.reshape(rows)


def solution(mesh):
    in_specs = (P("dp", None), P("dp"), P("dp"))
    out_specs = P("dp")
    return jax.shard_map(
        on_device, mesh=mesh, in_specs=in_specs, out_specs=out_specs, check_vma=False
    )
```

time: 376 us -> 131 us (0.35)
  waiting for transfers between devices: 183 us -> 14 us
  other arithmetic: 52.6 us -> 0.67 us
  local copies, waits for them, and re-layouts: 41.9 us -> 1.62 us
  blocking collectives: 58.7 us -> 82.2 us
  Pallas kernels: 0 us -> 19.5 us
  starting transfers between devices: 29.5 us -> 11.2 us
  matrix products: 7.09 us -> 0 us
    all_to_all x2 -> x0, waiting for transfers between devices: 183 us -> none  [the longest x1 183 us: on_device(): lax.all_to_all(outgoing, 'dp', split_axis=0, concat_axis=0, tiled=True)]
    all_to_all x2 -> x0, starting transfers between devices: 29.5 us -> none  [the longest x1 17.1 us: on_device(): lax.all_to_all(outgoing_ids, 'dp', split_axis=0, concat_axis=0, tiled=True)]
    all_to_all x1 -> x2, blocking collectives: 34 us -> 58.9 us  [the longest x1 42 us: on_device(): lax.all_to_all(packed, 'dp', split_axis=0, concat_axis=0, tiled=True)]
    scatter x1 -> x0, other arithmetic: 24.1 us -> none  [on_device(): outgoing = jnp.zeros((owner_count * capacity, feature_count), jnp.bfloat1...]
    gather x1 -> x0, local copies, waits for them, and re-layouts: 23 us -> none  [on_device(): jnp.take(returned, jnp.minimum(target, owner_count * capacity - 1), axis=0)]
    pallas_call x0 -> x4, Pallas kernels: none -> 19.5 us  [the longest x1 8.85 us: on_device(): call(pack_kernel, (jax.ShapeDtypeStruct((ROWS, features + 128), jnp.bfloa...]
    another operation x3 -> x1, other arithmetic: 19 us -> 0.67 us  [on_device(): jnp.stack([tile, 2 * chip + 1 - core, 2 * ((chip + 3) % 4) + core, 2 * ((...]
    scatter x1 -> x0, local copies, waits for them, and re-layouts: 15.5 us -> none  [on_device(): jnp.full((owner_count * capacity,), -1, jnp.int32).at[target]]
  transfers between devices with their start and end apart: 2 -> 3, of which waited for: 1 -> 2; matrix products, arithmetic and copies ran while one was open for 8% -> 1% of each run, Pallas kernels for 0% -> 3%
where the time goes in v1:
time: 131 us; the launch traced here: 129 us
  blocking collectives  82.2 us (63%)
  Pallas kernels  19.5 us (15%)
  waiting for transfers between devices  14 us (11%)
  starting transfers between devices  11.2 us (9%)
  local copies, waits for them, and re-layouts  1.62 us (1%)
    all_to_all x1, blocking collectives, on_device(): lax.all_to_all(packed, 'dp', split_axis=0, concat_axis=0, tiled=True)  42 us
    pmax x1, blocking collectives, on_device(): best = lax.pmax(best, 'tile')  23.4 us
    all_to_all x1, blocking collectives, on_device(): best = lax.all_to_all(best, 'dp', split_axis=0, concat_axis=0, tiled=True)  16.8 us
    ppermute x1, waiting for transfers between devices, on_device(): n = lax.ppermute(a, 'tile', backward)  9.07 us
    pallas_call x1, Pallas kernels, on_device(): call(pack_kernel, (jax.ShapeDtypeStruct((ROWS, features + 128), jnp.bfloa...  8.85 us
    pallas_call x1, Pallas kernels, on_device(): call(cross_kernel, partial_shape, [smem, vmem, vmem, vmem, vmem, vmem, vm...  5.05 us
    ppermute x1, starting transfers between devices, on_device(): b = lax.ppermute(a, 'tile', swap)  4.97 us
    ppermute x1, waiting for transfers between devices, on_device(): p = lax.ppermute(a, 'tile', forward)  4.95 us
  transfers between devices with their start and end apart: 3, of which 2 were waited for; matrix products, arithmetic and copies ran while one was open for 1% of the time, Pallas kernels for 3%

profile of v1, /device:TPU:1, one launch (start us, length us, event | category | flops | bytes accessed | tf_op | source)
XLA Modules:
  0.0 129.3 jit_solution(17260063327094197204)
XLA Ops:
  0.0 8.8 %shard_map.37 = (bf16[512,896]{1,0:T(8,128)(2,1)}, s32[1,4096]{1,0:T(1,128)}) custom-call(s32[1]{0:T(128)} %bitcast.tile_ref, s32[1,4096]{1,0:T(1,128)} %bitcast.19, s32[1,4096]{1,0:T(1,128)} %bitcast.20, bf16[4096,768]{1,0:T(8,128)(2,1)} %emb_ref.1), custom_call_target="tpu_custom_call" | custom-call | bytes 1048576 | tf_op jit(solution)/shard_map/pallas_call | solution.py:146
  8.8 42.0 %all_to_all.17 = bf16[64,8,896]{2,1,0:T(8,128)(2,1)S(1)} all-to-all(bf16[64,8,896]{2,1,0:T(8,128)(2,1)} %bitcast.16), channel_id=1, replica_groups=mesh['dp'=64,'tile'=8] {'dp'}, dimensions={0} | all-to-all | bytes 1835008 | tf_op jit(solution)/shard_map/all_to_all | solution.py:156
  50.9 0.1 slice.13.a_ref
  50.9 0.0 copy-start
  50.9 5.0 %collective-permute-start = (bf16[512,768]{1,0:T(8,128)(2,1)S(1)}, bf16[512,768]{1,0:T(8,128)(2,1)S(1)}, u32[]{:S(2)}, u32[]{:S(2)}) collective-permute-start(bf16[512,768]{1,0:T(8,128)(2,1)S(1)} %slice.13.a_ref), channel_id=1, source_target_pairs={{0,1},{1,0},{2,3},{3,2},{4,5},{5,4},{6,7},{7,6},{8,9},{9,8},{10,11... | collective-permute-start | bytes 2359304 | tf_op jit(solution)/shard_map/ppermute | solution.py:164
  55.9 4.3 %collective-permute-start.2 = (bf16[512,768]{1,0:T(8,128)(2,1)S(1)}, bf16[512,768]{1,0:T(8,128)(2,1)S(1)}, u32[]{:S(2)}, u32[]{:S(2)}) collective-permute-start(bf16[512,768]{1,0:T(8,128)(2,1)S(1)} %slice.13.a_ref), channel_id=1, source_target_pairs={{2,0},{3,1},{4,2},{5,3},{7,4},{6,5},{1,6},{0,7},{10,8},{11,9},{12,... | collective-permute-start | bytes 2359304 | tf_op jit(solution)/shard_map/ppermute | solution.py:166
  60.2 1.9 %collective-permute-start.1 = (bf16[512,768]{1,0:T(8,128)(2,1)S(1)}, bf16[512,768]{1,0:T(8,128)(2,1)}, u32[]{:S(2)}, u32[]{:S(2)}) collective-permute-start(bf16[512,768]{1,0:T(8,128)(2,1)S(1)} %slice.13.a_ref), channel_id=1, source_target_pairs={{0,2},{1,3},{2,4},{3,5},{4,6},{5,7},{6,0},{7,1},{8,10},{9,11},{10,... | collective-permute-start | bytes 2359304 | tf_op jit(solution)/shard_map/ppermute | solution.py:165
  62.2 0.7 pad_add_fusion.groups_ref
  62.9 0.7 slice.12.tag_ref
  63.5 0.0 collective-permute-done.b_ref
  63.5 0.0 copy-done
  63.5 0.0 copy-start.1
  63.5 0.9 copy-done.1
  64.4 3.6 %shard_map.38.own_ref = f32[64,128]{1,0:T(8,128)} custom-call(s32[4]{0:T(128)} %pad_add_fusion.groups_ref, bf16[512,128]{1,0:T(8,128)(2,1)} %slice.12.tag_ref, bf16[512,768]{1,0:T(8,128)(2,1)} %copy-done, bf16[512,768]{1,0:T(8,128)(2,1)} %copy-done.1), custom_call_target="tpu_custom_call" | custom-call | flops 805306368 | bytes 1048576 | tf_op jit(solution)/shard_map/pallas_call | solution.py:176
  68.0 9.1 %collective-permute-done.2.n_ref = bf16[512,768]{1,0:T(8,128)(2,1)S(1)} collective-permute-done((bf16[512,768]{1,0:T(8,128)(2,1)S(1)}, bf16[512,768]{1,0:T(8,128)(2,1)S(1)}, u32[]{:S(2)}, u32[]{:S(2)}) %collective-permute-start.2) | collective-permute-done | bytes 786464 | tf_op jit(solution)/shard_map/ppermute | solution.py:166
  77.1 0.0 copy-start.2
  77.1 4.9 %collective-permute-done.1.p_ref = bf16[512,768]{1,0:T(8,128)(2,1)} collective-permute-done((bf16[512,768]{1,0:T(8,128)(2,1)S(1)}, bf16[512,768]{1,0:T(8,128)(2,1)}, u32[]{:S(2)}, u32[]{:S(2)}) %collective-permute-start.1) | collective-permute-done | bytes 786464 | tf_op jit(solution)/shard_map/ppermute | solution.py:165
  82.0 0.0 copy-done.2
  82.0 5.0 %shard_map.39 = f32[64,128]{1,0:T(8,128)} custom-call(s32[4]{0:T(128)} %pad_add_fusion.groups_ref, bf16[512,128]{1,0:T(8,128)(2,1)} %slice.12.tag_ref, f32[64,128]{1,0:T(8,128)} %shard_map.38.own_ref, bf16[512,768]{1,0:T(8,128)(2,1)} %copy-done, bf16[512,768]{1,0:T(8,128)(2,1)} %copy-done.1, bf16[512,768]{1,0:T(8,128)(2,1)} %collective-permute-done.1.p_ref, ...), custom_call_target="tpu_custom_call" | custom-call | flops 1207959552 | bytes 1048576 | tf_op jit(solution)/shard_map/pallas_call | solution.py:182
  87.1 16.8 %all_to_all.18 = f32[64,1,64]{2,1,0:T(1,128)S(1)} all-to-all(f32[64,1,64]{2,1,0:T(1,128)} %bitcast.18), channel_id=1, replica_groups=mesh['dp'=64,'tile'=8] {'dp'}, dimensions={0} | all-to-all | bytes 32768 | tf_op jit(solution)/shard_map/all_to_all | solution.py:189
  103.9 23.4 %pmax.7.best_ref = f32[64,64]{1,0:T(8,128)} all-reduce(f32[64,64]{1,0:T(8,128)S(1)} %bitcast.17), channel_id=1, replica_groups=mesh['dp'=64,'tile'=8] {'tile'}, use_global_device_ids=true, to_apply=%region_0.1 | all-reduce | flops 4096 | bytes 32768 | tf_op jit(solution)/shard_map/pmax | solution.py:190
  127.3 2.0 %shard_map.40 = f32[1,4096]{1,0:T(1,128)} custom-call(s32[1,4096]{1,0:T(1,128)} %get-tuple-element.7.place_ref, f32[64,64]{1,0:T(8,128)} %pmax.7.best_ref), custom_call_target="tpu_custom_call" | custom-call | bytes 1048576 | tf_op jit(solution)/shard_map/pallas_call | solution.py:191
Async XLA Ops:
  50.9 12.6 %copy-start = (bf16[512,768]{1,0:T(8,128)(2,1)}, bf16[512,768]{1,0:T(8,128)(2,1)S(1)}, u32[]{:S(2)}) copy-start(bf16[512,768]{1,0:T(8,128)(2,1)S(1)} %slice.13.a_ref) | copy-start | bytes 2359300
  50.9 12.6 %collective-permute-start = (bf16[512,768]{1,0:T(8,128)(2,1)S(1)}, bf16[512,768]{1,0:T(8,128)(2,1)S(1)}, u32[]{:S(2)}, u32[]{:S(2)}) collective-permute-start(bf16[512,768]{1,0:T(8,128)(2,1)S(1)} %slice.13.a_ref), channel_id=1, source_target_pairs={{0,1},{1,0},{2,3},{3,2},{4,5},{5,4},{6,7},{7,6},{8,9},{9,8},{10,11... | collective-permute-start | bytes 2359304 | tf_op jit(solution)/shard_map/ppermute | solution.py:164
  55.9 21.2 %collective-permute-start.2 = (bf16[512,768]{1,0:T(8,128)(2,1)S(1)}, bf16[512,768]{1,0:T(8,128)(2,1)S(1)}, u32[]{:S(2)}, u32[]{:S(2)}) collective-permute-start(bf16[512,768]{1,0:T(8,128)(2,1)S(1)} %slice.13.a_ref), channel_id=1, source_target_pairs={{2,0},{3,1},{4,2},{5,3},{7,4},{6,5},{1,6},{0,7},{10,8},{11,9},{12,... | collective-permute-start | bytes 2359304 | tf_op jit(solution)/shard_map/ppermute | solution.py:166
  60.2 21.8 %collective-permute-start.1 = (bf16[512,768]{1,0:T(8,128)(2,1)S(1)}, bf16[512,768]{1,0:T(8,128)(2,1)}, u32[]{:S(2)}, u32[]{:S(2)}) collective-permute-start(bf16[512,768]{1,0:T(8,128)(2,1)S(1)} %slice.13.a_ref), channel_id=1, source_target_pairs={{0,2},{1,3},{2,4},{3,5},{4,6},{5,7},{6,0},{7,1},{8,10},{9,11},{10,... | collective-permute-start | bytes 2359304 | tf_op jit(solution)/shard_map/ppermute | solution.py:165
  63.5 0.9 copy-start.1
  77.1 5.0 %copy-start.2 = (bf16[512,768]{1,0:T(8,128)(2,1)}, bf16[512,768]{1,0:T(8,128)(2,1)S(1)}, u32[]{:S(2)}) copy-start(bf16[512,768]{1,0:T(8,128)(2,1)S(1)} %collective-permute-done.2.n_ref) | copy-start | bytes 2359300

commit v2 on v1

v2 whole, which is shorter than its diff:
```python
import jax
import jax.numpy as jnp
from jax import lax
from jax.experimental import pallas as pl
from jax.experimental.pallas import tpu as pltpu
from jax.sharding import PartitionSpec as P

OWNERS = 64
CAPACITY = 64
TILES = 8
PART = CAPACITY // TILES
ROWS = OWNERS * PART
TAG = 2.0
NEXT_CROSSED = (0, 0, 0, 1)
PREVIOUS_CROSSED = (0, 1, 1, 1)
PLACE_FLOPS = 4_000_000_000
VMEM = 16 * 1024 * 1024


def iota(shape, dim):
    return lax.broadcasted_iota(jnp.int32, shape, dim)


def nt_dot(a, b):
    return lax.dot_general(a, b, (((1,), (1,)), ((), ())), preferred_element_type=jnp.float32)


def one_hot(flags):
    return jnp.where(flags, jnp.float32(1), jnp.float32(0)).astype(jnp.bfloat16)


def place_kernel(tile_ref, labels_ref, place_ref, wanted_ref, tag_ref, tags):
    rows = labels_ref.shape[1]
    width = 256
    labels = labels_ref[...]
    owner = jnp.where(labels >= 0, labels & (OWNERS - 1), -1)
    member_hot = one_hot(owner == iota((OWNERS, rows), 0))
    strictly_before = one_hot(iota((width, width), 0) < iota((width, width), 1))
    carry = jnp.zeros((OWNERS, 1), jnp.float32)
    slots = []
    for start in range(0, rows, width):
        block = member_hot[:, start : start + width]
        rank = carry + jnp.dot(block, strictly_before, preferred_element_type=jnp.float32)
        block = block.astype(jnp.float32)
        slots.append(jnp.sum(block * rank, axis=0, keepdims=True))
        carry = carry + jnp.sum(block, axis=1, keepdims=True)
    slot = jnp.concatenate(slots, axis=1).astype(jnp.int32)
    place_ref[...] = jnp.where(owner >= 0, owner * CAPACITY + slot, -1)
    part = slot >> 3
    local = slot & (PART - 1)
    wanted_ref[...] = jnp.where((owner >= 0) & (part == tile_ref[0]), owner * PART + local, -1)
    marks = TILES * 4
    mark = jnp.where(owner >= 0, local * marks + part * 4 + (labels >> 6), -1)
    mark_hot = one_hot(iota((PART * marks, rows), 0) == mark)
    by_owner = TAG * nt_dot(member_hot, mark_hot)
    tags[...] = jnp.zeros(tags.shape, jnp.float32)
    for i in range(PART):
        tags[:, i, :marks] = by_owner[:, i * marks : (i + 1) * marks]
    tag_ref[...] = tags[...].reshape(ROWS, 128).astype(jnp.bfloat16)


def pack_kernel(wanted_ref, tag_ref, emb_ref, unit_ref):
    rows, features = emb_ref.shape
    pick = one_hot(iota((ROWS, rows), 0) == wanted_ref[...])
    total = jnp.dot(pick, emb_ref[...], preferred_element_type=jnp.float32)
    scale = lax.rsqrt(jnp.sum(total * total, axis=1, keepdims=True) + 1e-06)
    unit_ref[:, :features] = (total * scale).astype(jnp.bfloat16)
    unit_ref[:, features:] = tag_ref[...]


def marks_of(tag, group):
    lane, mark = iota((128, 128), 0), iota((128, 128), 1)
    take = one_hot((lane == group * 4 + mark) & (mark < 4))
    return jnp.dot(tag, take, preferred_element_type=jnp.float32).astype(jnp.bfloat16)


def spread(best, group):
    row, lane = iota((ROWS, 128), 0), iota((ROWS, 128), 1)
    value = jnp.maximum(best - TAG * TAG, -1.0)
    placed = jnp.where(lane == group * PART + row % PART, value, -2.0)
    return jnp.max(placed.reshape(OWNERS, PART, 128), axis=1)


def row_best(scores):
    return jnp.max(scores, axis=1, keepdims=True)


def column_best(scores):
    best = jnp.max(scores.reshape(scores.shape[0] // 8, 8, ROWS), axis=0)
    best = jnp.max(best, axis=0, keepdims=True)
    return jnp.broadcast_to(best, (128, ROWS)).T[:, :1]


def own_kernel(groups_ref, tag_ref, a_ref, out_ref):
    marks_a = marks_of(tag_ref[...], groups_ref[0])
    a = a_ref[...]
    same = nt_dot(a, a) + nt_dot(marks_a, marks_a)
    same = jnp.where(iota((ROWS, ROWS), 0) == iota((ROWS, ROWS), 1), -2.0, same)
    out_ref[...] = spread(row_best(same), groups_ref[0])


def previous_kernel(groups_ref, tag_ref, best_ref, a_ref, p_ref, out_ref):
    tag = tag_ref[...]
    marks_a, marks_p = marks_of(tag, groups_ref[0]), marks_of(tag, groups_ref[2])
    scores = nt_dot(a_ref[...], p_ref[...]) + nt_dot(marks_a, marks_p)
    best = jnp.maximum(best_ref[...], spread(row_best(scores), groups_ref[0]))
    out_ref[...] = jnp.maximum(best, spread(column_best(scores), groups_ref[2]))


def last_kernel(groups_ref, tag_ref, best_ref, a_ref, b_ref, p_ref, n_ref, out_ref):
    tag = tag_ref[...]
    a, n = a_ref[...], n_ref[...]
    marks_a, marks_n = marks_of(tag, groups_ref[0]), marks_of(tag, groups_ref[3])
    a_b = nt_dot(a, b_ref[...]) + nt_dot(marks_a, marks_of(tag, groups_ref[1]))
    a_n = nt_dot(a, n) + nt_dot(marks_a, marks_n)
    p_n = nt_dot(p_ref[...], n) + nt_dot(marks_of(tag, groups_ref[2]), marks_n)
    best = jnp.maximum(best_ref[...], spread(row_best(jnp.maximum(a_n, a_b)), groups_ref[0]))
    best = jnp.maximum(best, spread(row_best(p_n), groups_ref[2]))
    out_ref[...] = jnp.maximum(best, spread(column_best(jnp.maximum(a_n, p_n)), groups_ref[3]))


def pick_kernel(place_ref, best_ref, out_ref):
    place = place_ref[...]
    rows = place.shape[1]
    owner_hot = one_hot(place // CAPACITY == iota((OWNERS, rows), 0))
    best = jnp.max(best_ref[...], axis=0)
    best = best.T[:CAPACITY]
    high = best.astype(jnp.bfloat16)
    rest = best - high.astype(jnp.float32)
    middle = rest.astype(jnp.bfloat16)
    low = (rest - middle.astype(jnp.float32)).astype(jnp.bfloat16)
    by_slot = (
        jnp.dot(high, owner_hot, preferred_element_type=jnp.float32)
        + jnp.dot(middle, owner_hot, preferred_element_type=jnp.float32)
        + jnp.dot(low, owner_hot, preferred_element_type=jnp.float32)
    )
    here = place % CAPACITY == iota((CAPACITY, rows), 0)
    picked = jnp.sum(jnp.where(here, by_slot, 0.0), axis=0, keepdims=True)
    out_ref[...] = jnp.where(place >= 0, picked, -1.0)


def call(kernel, out_shape, in_specs, flops=0, scratch=()):
    return pl.pallas_call(
        kernel,
        out_shape=out_shape,
        in_specs=in_specs,
        scratch_shapes=list(scratch),
        compiler_params=pltpu.CompilerParams(vmem_limit_bytes=VMEM),
        cost_estimate=pl.CostEstimate(flops=flops, bytes_accessed=1 << 20, transcendentals=0),
    )


VMEM_SPEC = pl.BlockSpec(memory_space=pltpu.VMEM)
SMEM_SPEC = pl.BlockSpec(memory_space=pltpu.SMEM)
PARTIAL = jax.ShapeDtypeStruct((OWNERS, 128), jnp.float32)


def pack(tile, cluster_ids, padding, embeddings):
    rows, features = embeddings.shape
    labels = jnp.where(padding == 0, cluster_ids, -1).reshape(1, rows)
    row = jax.ShapeDtypeStruct((1, rows), jnp.int32)
    place, wanted, tag = call(
        place_kernel,
        (row, row, jax.ShapeDtypeStruct((ROWS, 128), jnp.bfloat16)),
        [SMEM_SPEC, VMEM_SPEC],
        flops=PLACE_FLOPS,
        scratch=[pltpu.VMEM((OWNERS, PART, 128), jnp.float32)],
    )(tile.reshape(1), labels)
    packed = call(
        pack_kernel,
        jax.ShapeDtypeStruct((ROWS, features + 128), jnp.bfloat16),
        [VMEM_SPEC] * 3,
        flops=2 * ROWS * rows * features,
    )(wanted, tag, embeddings)
    return packed, place


def scores(kernel, groups, *arrays):
    flops = 4 * ROWS * ROWS * arrays[-1].shape[1]
    specs = [SMEM_SPEC] + [VMEM_SPEC] * len(arrays)
    return call(kernel, PARTIAL, specs, flops)(groups, *arrays)


def pick(place, best):
    out_shape = jax.ShapeDtypeStruct(place.shape, jnp.float32)
    return call(pick_kernel, out_shape, [VMEM_SPEC] * 2)(place, best)


def on_device(embeddings, cluster_ids, padding):
    rows, features = embeddings.shape
    tile = lax.axis_index("tile")
    chip, core = tile // 2, tile % 2
    groups = jnp.stack(
        [
            tile,
            2 * chip + 1 - core,
            2 * ((chip + 3) % 4) + jnp.where(chip > 0, 1 - core, core),
            2 * ((chip + 1) % 4) + jnp.where(chip == 3, 1 - core, core),
        ]
    ).astype(jnp.int32)
    packed, place = pack(tile, cluster_ids, padding, embeddings)
    packed = packed.reshape(OWNERS, PART, features + 128)
    received = lax.all_to_all(packed, "dp", split_axis=0, concat_axis=0, tiled=True)
    received = received.reshape(ROWS, features + 128)
    a, tag = lax.optimization_barrier((received[:, :features], received[:, features:]))
    swap = [(2 * x + c, 2 * x + 1 - c) for x in range(4) for c in range(2)]
    backward = [
        (2 * ((x + 1) % 4) + c, 2 * x + (c ^ NEXT_CROSSED[x])) for x in range(4) for c in range(2)
    ]
    forward = [
        (2 * ((x + 3) % 4) + c, 2 * x + (c ^ PREVIOUS_CROSSED[x]))
        for x in range(4)
        for c in range(2)
    ]
    p = lax.ppermute(a, "tile", forward)
    n = lax.ppermute(a, "tile", backward)
    b = lax.ppermute(a, "tile", swap)
    best = scores(own_kernel, groups, tag, a)
    best = scores(previous_kernel, groups, tag, best, a, p)
    best = scores(last_kernel, groups, tag, best, a, b, p, n)
    best = lax.all_to_all(best, "dp", split_axis=0, concat_axis=0, tiled=True)
    best = jnp.broadcast_to(best[None], (TILES, OWNERS, 128))
    best = lax.all_to_all(best, "tile", split_axis=0, concat_axis=0, tiled=True)
    return pick(place, best).reshape(rows)


def solution(mesh):
    in_specs = (P("dp", None), P("dp"), P("dp"))
    out_specs = P("dp")
    return jax.shard_map(
        on_device, mesh=mesh, in_specs=in_specs, out_specs=out_specs, check_vma=False
    )
```

time: 131 us -> 109 us (0.83); the launches traced: 129 us -> 109 us
  blocking collectives: 82.2 us -> 71 us
  Pallas kernels: 19.5 us -> 12.8 us
  waiting for transfers between devices: 14 us -> 11.6 us
    pmax x1 -> x0, blocking collectives: 23.4 us -> none  [on_device(): best = lax.pmax(best, 'tile')]
    all_to_all x0 -> x1, blocking collectives: none -> 12.3 us  [on_device(): best = lax.all_to_all(best, 'tile', split_axis=0, concat_axis=0, tiled=True)]
    pallas_call x4 -> x6, Pallas kernels: 19.5 us -> 12.8 us  [the longest x3 6.21 us: scores(): return call(kernel, PARTIAL, specs, flops)(groups, *arrays)]
    ppermute x1, waiting for transfers between devices: 9.07 us -> 2.39 us  [on_device(): n = lax.ppermute(a, 'tile', backward)]
    ppermute x1, waiting for transfers between devices: 4.95 us -> 9.19 us  [on_device(): p = lax.ppermute(a, 'tile', forward)]
    ppermute x1, starting transfers between devices: 1.92 us -> 5.97 us  [on_device(): p = lax.ppermute(a, 'tile', forward)]
    ppermute x1, starting transfers between devices: 4.97 us -> 1.92 us  [on_device(): b = lax.ppermute(a, 'tile', swap)]
  transfers between devices with their start and end apart: 3 -> 3, of which waited for: 2 -> 2; matrix products, arithmetic and copies ran while one was open for 1% -> 0% of each run, Pallas kernels for 3% -> 3%
where the time goes in v2:
time: 109 us
  blocking collectives  71 us (65%)
  Pallas kernels  12.8 us (12%)
  waiting for transfers between devices  11.6 us (11%)
  starting transfers between devices  11.5 us (11%)
    all_to_all x1, blocking collectives, on_device(): lax.all_to_all(packed, 'dp', split_axis=0, concat_axis=0, tiled=True)  41.9 us
    all_to_all x1, blocking collectives, on_device(): best = lax.all_to_all(best, 'dp', split_axis=0, concat_axis=0, tiled=True)  16.8 us
    all_to_all x1, blocking collectives, on_device(): best = lax.all_to_all(best, 'tile', split_axis=0, concat_axis=0, tiled=True)  12.3 us
    ppermute x1, waiting for transfers between devices, on_device(): p = lax.ppermute(a, 'tile', forward)  9.19 us
    pallas_call x3, Pallas kernels, scores(): return call(kernel, PARTIAL, specs, flops)(groups, *arrays)  6.21 us
    ppermute x1, starting transfers between devices, on_device(): p = lax.ppermute(a, 'tile', forward)  5.97 us
    ppermute x1, starting transfers between devices, on_device(): n = lax.ppermute(a, 'tile', backward)  3.65 us
    pallas_call x1, Pallas kernels, pack(): call(pack_kernel, jax.ShapeDtypeStruct((ROWS, features + 128), jnp.bfloat...  3.51 us
  transfers between devices with their start and end apart: 3, of which 2 were waited for; matrix products, arithmetic and copies ran while one was open for 0% of the time, Pallas kernels for 3%

profile of v2, /device:TPU:1, one launch (start us, length us, event | category | flops | bytes accessed | tf_op | source)
XLA Modules:
  0.0 108.9 jit_solution(5568136405384833701)
XLA Ops:
  0.0 0.7 compare_select_fusion
  0.7 0.0 copy-start
  0.7 1.8 %shard_map.37 = (s32[1,4096]{1,0:T(1,128)S(1)}, s32[1,4096]{1,0:T(1,128)S(1)}, bf16[512,128]{1,0:T(8,128)(2,1)S(1)}) custom-call(s32[1]{0:T(128)} %bitcast.tile_ref, s32[1,4096]{1,0:T(1,128)S(1)} %bitcast.14), custom_call_target="tpu_custom_call" | custom-call | flops 4000000000 | bytes 1048576 | tf_op jit(solution)/shard_map/pallas_call | solution.py:162
  2.5 1.0 copy-done
  3.5 3.5 %shard_map.38 = bf16[512,896]{1,0:T(8,128)(2,1)S(1)} custom-call(s32[1,4096]{1,0:T(1,128)S(1)} %get-tuple-element.11.wanted_ref, bf16[512,128]{1,0:T(8,128)(2,1)S(1)} %get-tuple-element.12.tag_ref, bf16[4096,768]{1,0:T(8,128)(2,1)S(1)} %copy-done), custom_call_target="tpu_custom_call" | custom-call | flops 3221225472 | bytes 1048576 | tf_op jit(solution)/shard_map/pallas_call | solution.py:169
  7.0 41.9 %all_to_all.19 = bf16[64,8,896]{2,1,0:T(8,128)(2,1)S(1)} all-to-all(bf16[64,8,896]{2,1,0:T(8,128)(2,1)S(1)} %bitcast.12), channel_id=1, replica_groups=mesh['dp'=64,'tile'=8] {'dp'}, dimensions={0} | all-to-all | bytes 1835008 | tf_op jit(solution)/shard_map/all_to_all | solution.py:203
  49.0 0.1 slice.8.a_ref
  49.0 6.0 %collective-permute-start = (bf16[512,768]{1,0:T(8,128)(2,1)S(1)}, bf16[512,768]{1,0:T(8,128)(2,1)S(1)}, u32[]{:S(2)}, u32[]{:S(2)}) collective-permute-start(bf16[512,768]{1,0:T(8,128)(2,1)S(1)} %slice.8.a_ref), channel_id=1, source_target_pairs={{6,0},{7,1},{0,3},{1,2},{2,5},{3,4},{4,7},{5,6},{14,8},{15,9},{8,1... | collective-permute-start | bytes 2359304 | tf_op jit(solution)/shard_map/ppermute | solution.py:215
  55.0 3.7 %collective-permute-start.2 = (bf16[512,768]{1,0:T(8,128)(2,1)S(1)}, bf16[512,768]{1,0:T(8,128)(2,1)S(1)}, u32[]{:S(2)}, u32[]{:S(2)}) collective-permute-start(bf16[512,768]{1,0:T(8,128)(2,1)S(1)} %slice.8.a_ref), channel_id=1, source_target_pairs={{2,0},{3,1},{4,2},{5,3},{6,4},{7,5},{0,7},{1,6},{10,8},{11,9},{12,... | collective-permute-start | bytes 2359304 | tf_op jit(solution)/shard_map/ppermute | solution.py:216
  58.7 1.9 %collective-permute-start.1 = (bf16[512,768]{1,0:T(8,128)(2,1)S(1)}, bf16[512,768]{1,0:T(8,128)(2,1)S(1)}, u32[]{:S(2)}, u32[]{:S(2)}) collective-permute-start(bf16[512,768]{1,0:T(8,128)(2,1)S(1)} %slice.8.a_ref), channel_id=1, source_target_pairs={{0,1},{1,0},{2,3},{3,2},{4,5},{5,4},{6,7},{7,6},{8,9},{9,8},{10,11... | collective-permute-start | bytes 2359304 | tf_op jit(solution)/shard_map/ppermute | solution.py:217
  60.7 0.1 pad_add_fusion.groups_ref
  60.7 1.5 %shard_map.39.best_ref = f32[64,128]{1,0:T(8,128)S(1)} custom-call(s32[4]{0:T(128)S(1)} %pad_add_fusion.groups_ref, bf16[512,128]{1,0:T(8,128)(2,1)S(1)} %slice.9.tag_ref, bf16[512,768]{1,0:T(8,128)(2,1)S(1)} %slice.8.a_ref), custom_call_target="tpu_custom_call" | custom-call | flops 805306368 | bytes 1048576 | tf_op jit(solution)/shard_map/pallas_call | solution.py:181
  62.3 9.2 %collective-permute-done.p_ref = bf16[512,768]{1,0:T(8,128)(2,1)S(1)} collective-permute-done((bf16[512,768]{1,0:T(8,128)(2,1)S(1)}, bf16[512,768]{1,0:T(8,128)(2,1)S(1)}, u32[]{:S(2)}, u32[]{:S(2)}) %collective-permute-start) | collective-permute-done | bytes 786464 | tf_op jit(solution)/shard_map/ppermute | solution.py:215
  71.5 1.7 %shard_map.40.best_ref = f32[64,128]{1,0:T(8,128)S(1)} custom-call(s32[4]{0:T(128)S(1)} %pad_add_fusion.groups_ref, bf16[512,128]{1,0:T(8,128)(2,1)S(1)} %slice.9.tag_ref, f32[64,128]{1,0:T(8,128)S(1)} %shard_map.39.best_ref, bf16[512,768]{1,0:T(8,128)(2,1)S(1)} %slice.8.a_ref, bf16[512,768]{1,0:T(8,128)(2,1)S(1)} %collective-permute-done.p_ref), custom_call_target="tpu_custom_call" | custom-call | flops 805306368 | bytes 1048576 | tf_op jit(solution)/shard_map/pallas_call | solution.py:181
  73.2 2.4 %collective-permute-done.2.n_ref = bf16[512,768]{1,0:T(8,128)(2,1)S(1)} collective-permute-done((bf16[512,768]{1,0:T(8,128)(2,1)S(1)}, bf16[512,768]{1,0:T(8,128)(2,1)S(1)}, u32[]{:S(2)}, u32[]{:S(2)}) %collective-permute-start.2) | collective-permute-done | bytes 786464 | tf_op jit(solution)/shard_map/ppermute | solution.py:216
  75.6 0.0 collective-permute-done.1.b_ref
  75.6 3.0 %shard_map.41 = f32[64,128]{1,0:T(8,128)S(1)} custom-call(s32[4]{0:T(128)S(1)} %pad_add_fusion.groups_ref, bf16[512,128]{1,0:T(8,128)(2,1)S(1)} %slice.9.tag_ref, f32[64,128]{1,0:T(8,128)S(1)} %shard_map.40.best_ref, bf16[512,768]{1,0:T(8,128)(2,1)S(1)} %slice.8.a_ref, bf16[512,768]{1,0:T(8,128)(2,1)S(1)} %collective-permute-done.1.b_ref, ...), custom_call_target="tpu_custom_call" | custom-call | flops 805306368 | bytes 1048576 | tf_op jit(solution)/shard_map/pallas_call | solution.py:181
  78.6 16.8 %all_to_all.20 = f32[64,1,128]{2,1,0:T(1,128)S(1)} all-to-all(f32[64,1,128]{2,1,0:T(1,128)S(1)} %bitcast.13), channel_id=1, replica_groups=mesh['dp'=64,'tile'=8] {'dp'}, dimensions={0} | all-to-all | bytes 65536 | tf_op jit(solution)/shard_map/all_to_all | solution.py:221
  95.4 12.3 %all_to_all.21.best_ref = f32[8,64,128]{2,1,0:T(8,128)S(1)} all-to-all(f32[8,64,128]{2,1,0:T(8,128)S(1)} %broadcast_in_dim.14), channel_id=1, replica_groups=mesh['dp'=64,'tile'=8] {'tile'}, dimensions={0} | all-to-all | bytes 524288 | tf_op jit(solution)/shard_map/all_to_all | solution.py:223
  107.7 1.3 %shard_map.42 = f32[1,4096]{1,0:T(1,128)} custom-call(s32[1,4096]{1,0:T(1,128)S(1)} %get-tuple-element.10.place_ref, f32[8,64,128]{2,1,0:T(8,128)S(1)} %all_to_all.21.best_ref), custom_call_target="tpu_custom_call" | custom-call | bytes 1048576 | tf_op jit(solution)/shard_map/pallas_call | solution.py:186
  (2 shorter events, 0.0 us)
Async XLA Ops:
  0.7 2.8 %copy-start = (bf16[4096,768]{1,0:T(8,128)(2,1)S(1)}, bf16[4096,768]{1,0:T(8,128)(2,1)}, u32[]{:S(2)}) copy-start(bf16[4096,768]{1,0:T(8,128)(2,1)} %emb_ref.1) | copy-start | bytes 18874372
  49.0 22.4 %collective-permute-start = (bf16[512,768]{1,0:T(8,128)(2,1)S(1)}, bf16[512,768]{1,0:T(8,128)(2,1)S(1)}, u32[]{:S(2)}, u32[]{:S(2)}) collective-permute-start(bf16[512,768]{1,0:T(8,128)(2,1)S(1)} %slice.8.a_ref), channel_id=1, source_target_pairs={{6,0},{7,1},{0,3},{1,2},{2,5},{3,4},{4,7},{5,6},{14,8},{15,9},{8,1... | collective-permute-start | bytes 2359304 | tf_op jit(solution)/shard_map/ppermute | solution.py:215
  55.0 20.5 %collective-permute-start.2 = (bf16[512,768]{1,0:T(8,128)(2,1)S(1)}, bf16[512,768]{1,0:T(8,128)(2,1)S(1)}, u32[]{:S(2)}, u32[]{:S(2)}) collective-permute-start(bf16[512,768]{1,0:T(8,128)(2,1)S(1)} %slice.8.a_ref), channel_id=1, source_target_pairs={{2,0},{3,1},{4,2},{5,3},{6,4},{7,5},{0,7},{1,6},{10,8},{11,9},{12,... | collective-permute-start | bytes 2359304 | tf_op jit(solution)/shard_map/ppermute | solution.py:216
  58.7 16.9 %collective-permute-start.1 = (bf16[512,768]{1,0:T(8,128)(2,1)S(1)}, bf16[512,768]{1,0:T(8,128)(2,1)S(1)}, u32[]{:S(2)}, u32[]{:S(2)}) collective-permute-start(bf16[512,768]{1,0:T(8,128)(2,1)S(1)} %slice.8.a_ref), channel_id=1, source_target_pairs={{0,1},{1,0},{2,3},{3,2},{4,5},{5,4},{6,7},{7,6},{8,9},{9,8},{10,11... | collective-permute-start | bytes 2359304 | tf_op jit(solution)/shard_map/ppermute | solution.py:217

commit v3 on v2

--- a/solution.py
+++ b/solution.py
@@ -13,7 +13,7 @@
 TAG = 2.0
 NEXT_CROSSED = (0, 0, 0, 1)
 PREVIOUS_CROSSED = (0, 1, 1, 1)
-PLACE_FLOPS = 4_000_000_000
+PLACE_FLOPS = 2_000_000_000
 VMEM = 16 * 1024 * 1024
 
 
@@ -77,8 +77,9 @@
 def spread(best, group):
     row, lane = iota((ROWS, 128), 0), iota((ROWS, 128), 1)
     value = jnp.maximum(best - TAG * TAG, -1.0)
-    placed = jnp.where(lane == group * PART + row % PART, value, -2.0)
-    return jnp.max(placed.reshape(OWNERS, PART, 128), axis=1)
+    here = lane == group * PART + (row & 7) + ((row >> 5) & 1) * CAPACITY
+    placed = jnp.where(here, value, -2.0).reshape(8, 2, 4, PART, 128)
+    return jnp.max(jnp.max(placed, axis=1), axis=2).reshape(32, 128)
 
 
 def row_best(scores):
@@ -91,29 +92,34 @@
     return jnp.broadcast_to(best, (128, ROWS)).T[:, :1]
 
 
-def own_kernel(groups_ref, tag_ref, a_ref, out_ref):
-    marks_a = marks_of(tag_ref[...], groups_ref[0])
+def own_kernel(groups_ref, tag_ref, a_ref, out_ref, marks_ref):
+    tag = tag_ref[...]
+    for j in range(4):
+        marks_ref[j * ROWS : (j + 1) * ROWS, :] = marks_of(tag, groups_ref[j])
+    marks_a = marks_ref[:ROWS, :]
     a = a_ref[...]
     same = nt_dot(a, a) + nt_dot(marks_a, marks_a)
     same = jnp.where(iota((ROWS, ROWS), 0) == iota((ROWS, ROWS), 1), -2.0, same)
     out_ref[...] = spread(row_best(same), groups_ref[0])
 
 
-def previous_kernel(groups_ref, tag_ref, best_ref, a_ref, p_ref, out_ref):
-    tag = tag_ref[...]
-    marks_a, marks_p = marks_of(tag, groups_ref[0]), marks_of(tag, groups_ref[2])
+def marks(marks_ref, j):
+    return marks_ref[j * ROWS : (j + 1) * ROWS, :]
+
+
+def previous_kernel(groups_ref, marks_ref, best_ref, a_ref, p_ref, out_ref):
+    marks_a, marks_p = marks(marks_ref, 0), marks(marks_ref, 2)
     scores = nt_dot(a_ref[...], p_ref[...]) + nt_dot(marks_a, marks_p)
     best = jnp.maximum(best_ref[...], spread(row_best(scores), groups_ref[0]))
     out_ref[...] = jnp.maximum(best, spread(column_best(scores), groups_ref[2]))
 
 
-def last_kernel(groups_ref, tag_ref, best_ref, a_ref, b_ref, p_ref, n_ref, out_ref):
-    tag = tag_ref[...]
+def last_kernel(groups_ref, marks_ref, best_ref, a_ref, b_ref, p_ref, n_ref, out_ref):
     a, n = a_ref[...], n_ref[...]
-    marks_a, marks_n = marks_of(tag, groups_ref[0]), marks_of(tag, groups_ref[3])
-    a_b = nt_dot(a, b_ref[...]) + nt_dot(marks_a, marks_of(tag, groups_ref[1]))
+    marks_a, marks_n = marks(marks_ref, 0), marks(marks_ref, 3)
+    a_b = nt_dot(a, b_ref[...]) + nt_dot(marks_a, marks(marks_ref, 1))
     a_n = nt_dot(a, n) + nt_dot(marks_a, marks_n)
-    p_n = nt_dot(p_ref[...], n) + nt_dot(marks_of(tag, groups_ref[2]), marks_n)
+    p_n = nt_dot(p_ref[...], n) + nt_dot(marks(marks_ref, 2), marks_n)
     best = jnp.maximum(best_ref[...], spread(row_best(jnp.maximum(a_n, a_b)), groups_ref[0]))
     best = jnp.maximum(best, spread(row_best(p_n), groups_ref[2]))
     out_ref[...] = jnp.maximum(best, spread(column_best(jnp.maximum(a_n, p_n)), groups_ref[3]))
@@ -122,9 +128,11 @@
 def pick_kernel(place_ref, best_ref, out_ref):
     place = place_ref[...]
     rows = place.shape[1]
-    owner_hot = one_hot(place // CAPACITY == iota((OWNERS, rows), 0))
-    best = jnp.max(best_ref[...], axis=0)
-    best = best.T[:CAPACITY]
+    owner = place >> 6
+    z, y = owner >> 3, owner & 7
+    owner_hot = one_hot(((z >> 2) << 5) + (y << 2) + (z & 3) == iota((OWNERS, rows), 0))
+    best = jnp.max(best_ref[...], axis=1).reshape(32, 128).T
+    best = jnp.concatenate([best[:CAPACITY], best[CAPACITY:]], axis=1)
     high = best.astype(jnp.bfloat16)
     rest = best - high.astype(jnp.float32)
     middle = rest.astype(jnp.bfloat16)
@@ -134,7 +142,7 @@
         + jnp.dot(middle, owner_hot, preferred_element_type=jnp.float32)
         + jnp.dot(low, owner_hot, preferred_element_type=jnp.float32)
     )
-    here = place % CAPACITY == iota((CAPACITY, rows), 0)
+    here = (place & (CAPACITY - 1)) == iota((CAPACITY, rows), 0)
     picked = jnp.sum(jnp.where(here, by_slot, 0.0), axis=0, keepdims=True)
     out_ref[...] = jnp.where(place >= 0, picked, -1.0)
 
@@ -152,7 +160,7 @@
 
 VMEM_SPEC = pl.BlockSpec(memory_space=pltpu.VMEM)
 SMEM_SPEC = pl.BlockSpec(memory_space=pltpu.SMEM)
-PARTIAL = jax.ShapeDtypeStruct((OWNERS, 128), jnp.float32)
+PARTIAL = jax.ShapeDtypeStruct((32, 128), jnp.float32)
 
 
 def pack(tile, cluster_ids, padding, embeddings):
@@ -175,15 +183,31 @@
     return packed, place
 
 
-def scores(kernel, groups, *arrays):
+def scores(kernel, groups, *arrays, out_shape=PARTIAL):
     flops = 4 * ROWS * ROWS * arrays[-1].shape[1]
     specs = [SMEM_SPEC] + [VMEM_SPEC] * len(arrays)
-    return call(kernel, PARTIAL, specs, flops)(groups, *arrays)
+    return call(kernel, out_shape, specs, flops)(groups, *arrays)
 
 
 def pick(place, best):
     out_shape = jax.ShapeDtypeStruct(place.shape, jnp.float32)
     return call(pick_kernel, out_shape, [VMEM_SPEC] * 2)(place, best)
+
+
+def exchange(array, axes):
+    sizes = dict(z=8, y=8, x=4, c=2)
+    strides = dict(z=64, y=8, x=2, c=1)
+    members, starts = [0], [0]
+    for axis in "zyxc":
+        steps = [i * strides[axis] for i in range(sizes[axis])]
+        if axis in axes:
+            members = [m + i for m in members for i in steps]
+        else:
+            starts = [m + i for m in starts for i in steps]
+    groups = [[start + m for m in members] for start in starts]
+    return lax.all_to_all(
+        array, ("dp", "tile"), split_axis=0, concat_axis=0, axis_index_groups=groups, tiled=True
+    )
 
 
 def on_device(embeddings, cluster_ids, padding):
@@ -215,12 +239,18 @@
     p = lax.ppermute(a, "tile", forward)
     n = lax.ppermute(a, "tile", backward)
     b = lax.ppermute(a, "tile", swap)
-    best = scores(own_kernel, groups, tag, a)
-    best = scores(previous_kernel, groups, tag, best, a, p)
-    best = scores(last_kernel, groups, tag, best, a, b, p, n)
-    best = lax.all_to_all(best, "dp", split_axis=0, concat_axis=0, tiled=True)
-    best = jnp.broadcast_to(best[None], (TILES, OWNERS, 128))
-    best = lax.all_to_all(best, "tile", split_axis=0, concat_axis=0, tiled=True)
+    marks_shape = jax.ShapeDtypeStruct((4 * ROWS, 128), jnp.bfloat16)
+    best, marks = scores(own_kernel, groups, tag, a, out_shape=(PARTIAL, marks_shape))
+    best = scores(previous_kernel, groups, marks, best, a, p)
+    best = scores(last_kernel, groups, marks, best, a, b, p, n)
+    best = jnp.broadcast_to(best.reshape(8, 1, 4, 128), (8, 2, 4, 128)).reshape(16, 4, 128)
+    best = exchange(best, "zc").reshape(8, 2, 4, 128)
+    best = jnp.max(best, axis=1)
+    best = jnp.concatenate([best[:, :, :CAPACITY], best[:, :, CAPACITY:]], axis=1)
+    best = best.transpose(1, 0, 2)
+    best = jnp.concatenate([best[:, :4], best[:, 4:]], axis=2)
+    best = jnp.broadcast_to(best[:, None], (8, 4, 4, 128)).reshape(32, 4, 128)
+    best = exchange(best, "yx").reshape(8, 4, 4, 128)
     return pick(place, best).reshape(rows)
 
 

time: 109 us -> 105 us (0.963)
  blocking collectives: 71 us -> 67.9 us
    all_to_all x2, blocking collectives: 29.1 us -> 26 us  [exchange(): lax.all_to_all(array, ('dp', 'tile'), split_axis=0, concat_axis=0, axis_i...]
where the time goes in v3:
time: 105 us
  blocking collectives  67.9 us (65%)
  Pallas kernels  12.3 us (12%)
  waiting for transfers between devices  11.7 us (11%)
  starting transfers between devices  11.5 us (11%)
  other arithmetic  1.07 us (1%)
    all_to_all x1, blocking collectives, on_device(): lax.all_to_all(packed, 'dp', split_axis=0, concat_axis=0, tiled=True)  41.9 us
    all_to_all x2, blocking collectives, exchange(): lax.all_to_all(array, ('dp', 'tile'), split_axis=0, concat_axis=0, axis_i...  26 us
    ppermute x1, waiting for transfers between devices, on_device(): p = lax.ppermute(a, 'tile', forward)  9.15 us
    ppermute x1, starting transfers between devices, on_device(): p = lax.ppermute(a, 'tile', forward)  5.97 us
    pallas_call x3, Pallas kernels, scores(): return call(kernel, out_shape, specs, flops)(groups, *arrays)  5.7 us
    ppermute x1, starting transfers between devices, on_device(): n = lax.ppermute(a, 'tile', backward)  3.65 us
    pallas_call x1, Pallas kernels, pack(): call(pack_kernel, jax.ShapeDtypeStruct((ROWS, features + 128), jnp.bfloat...  3.51 us
    ppermute x1, waiting for transfers between devices, on_device(): n = lax.ppermute(a, 'tile', backward)  2.57 us
  transfers between devices with their start and end apart: 3, of which 2 were waited for; matrix products, arithmetic and copies ran while one was open for 0% of the time, Pallas kernels for 3%

profile of v3, /device:TPU:1, one launch (start us, length us, event | category | flops | bytes accessed | tf_op | source)
XLA Modules:
  0.0 105.1 jit_solution(10103217486568787893)
XLA Ops:
  0.0 0.0 copy-start
  0.0 0.9 compare_select_fusion
  0.9 1.8 %shard_map.37 = (s32[1,4096]{1,0:T(1,128)S(1)}, s32[1,4096]{1,0:T(1,128)S(1)}, bf16[512,128]{1,0:T(8,128)(2,1)S(1)}) custom-call(s32[1]{0:T(128)} %bitcast.tile_ref, s32[1,4096]{1,0:T(1,128)S(1)} %bitcast.19), custom_call_target="tpu_custom_call" | custom-call | flops 2000000000 | bytes 1048576 | tf_op jit(solution)/shard_map/pallas_call | solution.py:170
  2.7 0.1 copy-done
  2.8 3.5 %shard_map.38 = bf16[512,896]{1,0:T(8,128)(2,1)S(1)} custom-call(s32[1,4096]{1,0:T(1,128)S(1)} %get-tuple-element.13.wanted_ref, bf16[512,128]{1,0:T(8,128)(2,1)S(1)} %get-tuple-element.14.tag_ref, bf16[4096,768]{1,0:T(8,128)(2,1)S(1)} %copy-done), custom_call_target="tpu_custom_call" | custom-call | flops 3221225472 | bytes 1048576 | tf_op jit(solution)/shard_map/pallas_call | solution.py:177
  6.3 41.9 %all_to_all.15 = bf16[64,8,896]{2,1,0:T(8,128)(2,1)S(1)} all-to-all(bf16[64,8,896]{2,1,0:T(8,128)(2,1)S(1)} %bitcast.16), channel_id=1, replica_groups=mesh['dp'=64,'tile'=8] {'dp'}, dimensions={0} | all-to-all | bytes 1835008 | tf_op jit(solution)/shard_map/all_to_all | solution.py:227
  48.3 0.1 slice.24.a_ref
  48.3 6.0 %collective-permute-start = (bf16[512,768]{1,0:T(8,128)(2,1)S(1)}, bf16[512,768]{1,0:T(8,128)(2,1)S(1)}, u32[]{:S(2)}, u32[]{:S(2)}) collective-permute-start(bf16[512,768]{1,0:T(8,128)(2,1)S(1)} %slice.24.a_ref), channel_id=1, source_target_pairs={{6,0},{7,1},{0,3},{1,2},{2,5},{3,4},{4,7},{5,6},{14,8},{15,9},{8,1... | collective-permute-start | bytes 2359304 | tf_op jit(solution)/shard_map/ppermute | solution.py:239
  54.3 3.7 %collective-permute-start.2 = (bf16[512,768]{1,0:T(8,128)(2,1)S(1)}, bf16[512,768]{1,0:T(8,128)(2,1)S(1)}, u32[]{:S(2)}, u32[]{:S(2)}) collective-permute-start(bf16[512,768]{1,0:T(8,128)(2,1)S(1)} %slice.24.a_ref), channel_id=1, source_target_pairs={{2,0},{3,1},{4,2},{5,3},{6,4},{7,5},{0,7},{1,6},{10,8},{11,9},{12,... | collective-permute-start | bytes 2359304 | tf_op jit(solution)/shard_map/ppermute | solution.py:240
  58.0 1.9 %collective-permute-start.1 = (bf16[512,768]{1,0:T(8,128)(2,1)S(1)}, bf16[512,768]{1,0:T(8,128)(2,1)S(1)}, u32[]{:S(2)}, u32[]{:S(2)}) collective-permute-start(bf16[512,768]{1,0:T(8,128)(2,1)S(1)} %slice.24.a_ref), channel_id=1, source_target_pairs={{0,1},{1,0},{2,3},{3,2},{4,5},{5,4},{6,7},{7,6},{8,9},{9,8},{10,11... | collective-permute-start | bytes 2359304 | tf_op jit(solution)/shard_map/ppermute | solution.py:241
  60.0 0.1 pad_add_fusion.groups_ref
  60.0 1.6 %shard_map.39 = (f32[32,128]{1,0:T(8,128)S(1)}, bf16[2048,128]{1,0:T(8,128)(2,1)S(1)}) custom-call(s32[4]{0:T(128)S(1)} %pad_add_fusion.groups_ref, bf16[512,128]{1,0:T(8,128)(2,1)S(1)} %slice.25.tag_ref, bf16[512,768]{1,0:T(8,128)(2,1)S(1)} %slice.24.a_ref), custom_call_target="tpu_custom_call" | custom-call | flops 805306368 | bytes 1048576 | tf_op jit(solution)/shard_map/pallas_call | solution.py:189
  61.6 9.1 %collective-permute-done.p_ref = bf16[512,768]{1,0:T(8,128)(2,1)S(1)} collective-permute-done((bf16[512,768]{1,0:T(8,128)(2,1)S(1)}, bf16[512,768]{1,0:T(8,128)(2,1)S(1)}, u32[]{:S(2)}, u32[]{:S(2)}) %collective-permute-start) | collective-permute-done | bytes 786464 | tf_op jit(solution)/shard_map/ppermute | solution.py:239
  70.8 1.5 %shard_map.40.best_ref = f32[32,128]{1,0:T(8,128)S(1)} custom-call(s32[4]{0:T(128)S(1)} %pad_add_fusion.groups_ref, bf16[2048,128]{1,0:T(8,128)(2,1)S(1)} %get-tuple-element.17.marks_ref, f32[32,128]{1,0:T(8,128)S(1)} %get-tuple-element.18.best_ref, bf16[512,768]{1,0:T(8,128)(2,1)S(1)} %slice.24.a_ref, bf16[512,768]{1,0:T(8,128)(2,1)S(1)} %collective-permute-done.p_ref), custom_call_target="tpu_custom_call" | custom-call | flops 805306368 | bytes 1048576 | tf_op jit(solution)/shard_map/pallas_call | solution.py:189
  72.3 2.6 %collective-permute-done.2.n_ref = bf16[512,768]{1,0:T(8,128)(2,1)S(1)} collective-permute-done((bf16[512,768]{1,0:T(8,128)(2,1)S(1)}, bf16[512,768]{1,0:T(8,128)(2,1)S(1)}, u32[]{:S(2)}, u32[]{:S(2)}) %collective-permute-start.2) | collective-permute-done | bytes 786464 | tf_op jit(solution)/shard_map/ppermute | solution.py:240
  74.9 0.0 collective-permute-done.1.b_ref
  74.9 2.6 %shard_map.41 = f32[32,128]{1,0:T(8,128)S(1)} custom-call(s32[4]{0:T(128)S(1)} %pad_add_fusion.groups_ref, bf16[2048,128]{1,0:T(8,128)(2,1)S(1)} %get-tuple-element.17.marks_ref, f32[32,128]{1,0:T(8,128)S(1)} %shard_map.40.best_ref, bf16[512,768]{1,0:T(8,128)(2,1)S(1)} %slice.24.a_ref, bf16[512,768]{1,0:T(8,128)(2,1)S(1)} %collective-permute-done.1.b_ref, ...), custom_call_target="tpu_custom_call" | custom-call | flops 805306368 | bytes 1048576 | tf_op jit(solution)/shard_map/pallas_call | solution.py:189
  77.5 11.7 %all_to_all.16 = f32[16,4,128]{2,1,0:T(4,128)S(1)} all-to-all(f32[16,4,128]{2,1,0:T(4,128)S(1)} %bitcast.23), channel_id=1, replica_groups={{0,1,64,65,128,129,192,193,256,257,320,321,384,385,448,449},{2,3,66,67,..., dimensions={0} | all-to-all | bytes 65536 | tf_op jit(solution)/shard_map/all_to_all | solution.py:208
  89.2 0.1 fusion.1
  89.3 0.1 pad_maximum_fusion
  89.4 14.3 %all_to_all.17 = f32[32,4,128]{2,1,0:T(4,128)S(1)} all-to-all(f32[32,4,128]{2,1,0:T(4,128)S(1)} %bitcast.22), channel_id=1, replica_groups={{0,2,4,6,8,10,12,14,16,18,20,22,24,26,28,30,32,34,36,38,40,42,44,46,48,..., dimensions={0} | all-to-all | bytes 131072 | tf_op jit(solution)/shard_map/all_to_all | solution.py:208
  103.7 1.4 %shard_map.42 = f32[1,4096]{1,0:T(1,128)} custom-call(s32[1,4096]{1,0:T(1,128)S(1)} %get-tuple-element.12.place_ref, f32[8,4,4,128]{3,2,1,0:T(4,128)S(1)} %bitcast.17), custom_call_target="tpu_custom_call" | custom-call | bytes 1048576 | tf_op jit(solution)/shard_map/pallas_call | solution.py:194
  (8 shorter events, 0.1 us)
Async XLA Ops:
  0.0 2.8 %copy-start = (bf16[4096,768]{1,0:T(8,128)(2,1)S(1)}, bf16[4096,768]{1,0:T(8,128)(2,1)}, u32[]{:S(2)}) copy-start(bf16[4096,768]{1,0:T(8,128)(2,1)} %emb_ref.1) | copy-start | bytes 18874372
  48.3 22.4 %collective-permute-start = (bf16[512,768]{1,0:T(8,128)(2,1)S(1)}, bf16[512,768]{1,0:T(8,128)(2,1)S(1)}, u32[]{:S(2)}, u32[]{:S(2)}) collective-permute-start(bf16[512,768]{1,0:T(8,128)(2,1)S(1)} %slice.24.a_ref), channel_id=1, source_target_pairs={{6,0},{7,1},{0,3},{1,2},{2,5},{3,4},{4,7},{5,6},{14,8},{15,9},{8,1... | collective-permute-start | bytes 2359304 | tf_op jit(solution)/shard_map/ppermute | solution.py:239
  54.3 20.5 %collective-permute-start.2 = (bf16[512,768]{1,0:T(8,128)(2,1)S(1)}, bf16[512,768]{1,0:T(8,128)(2,1)S(1)}, u32[]{:S(2)}, u32[]{:S(2)}) collective-permute-start(bf16[512,768]{1,0:T(8,128)(2,1)S(1)} %slice.24.a_ref), channel_id=1, source_target_pairs={{2,0},{3,1},{4,2},{5,3},{6,4},{7,5},{0,7},{1,6},{10,8},{11,9},{12,... | collective-permute-start | bytes 2359304 | tf_op jit(solution)/shard_map/ppermute | solution.py:240
  58.0 16.9 %collective-permute-start.1 = (bf16[512,768]{1,0:T(8,128)(2,1)S(1)}, bf16[512,768]{1,0:T(8,128)(2,1)S(1)}, u32[]{:S(2)}, u32[]{:S(2)}) collective-permute-start(bf16[512,768]{1,0:T(8,128)(2,1)S(1)} %slice.24.a_ref), channel_id=1, source_target_pairs={{0,1},{1,0},{2,3},{3,2},{4,5},{5,4},{6,7},{7,6},{8,9},{9,8},{10,11... | collective-permute-start | bytes 2359304 | tf_op jit(solution)/shard_map/ppermute | solution.py:241

commit v4 on v3

--- a/solution.py
+++ b/solution.py
@@ -11,8 +11,6 @@
 PART = CAPACITY // TILES
 ROWS = OWNERS * PART
 TAG = 2.0
-NEXT_CROSSED = (0, 0, 0, 1)
-PREVIOUS_CROSSED = (0, 1, 1, 1)
 PLACE_FLOPS = 2_000_000_000
 VMEM = 16 * 1024 * 1024
 
@@ -49,13 +47,13 @@
     part = slot >> 3
     local = slot & (PART - 1)
     wanted_ref[...] = jnp.where((owner >= 0) & (part == tile_ref[0]), owner * PART + local, -1)
-    marks = TILES * 4
-    mark = jnp.where(owner >= 0, local * marks + part * 4 + (labels >> 6), -1)
-    mark_hot = one_hot(iota((PART * marks, rows), 0) == mark)
-    by_owner = TAG * nt_dot(member_hot, mark_hot)
+    cluster = jnp.where(owner >= 0, (labels >> 6) + 1, 0).astype(jnp.float32)
+    here = local * TILES + part == iota((CAPACITY, rows), 0)
+    slot_cluster = jnp.where(here, cluster, 0.0).astype(jnp.bfloat16)
+    by_owner = nt_dot(member_hot, slot_cluster)
     tags[...] = jnp.zeros(tags.shape, jnp.float32)
     for i in range(PART):
-        tags[:, i, :marks] = by_owner[:, i * marks : (i + 1) * marks]
+        tags[:, i, :TILES] = by_owner[:, i * TILES : (i + 1) * TILES]
     tag_ref[...] = tags[...].reshape(ROWS, 128).astype(jnp.bfloat16)
 
 
@@ -69,9 +67,10 @@
 
 
 def marks_of(tag, group):
-    lane, mark = iota((128, 128), 0), iota((128, 128), 1)
-    take = one_hot((lane == group * 4 + mark) & (mark < 4))
-    return jnp.dot(tag, take, preferred_element_type=jnp.float32).astype(jnp.bfloat16)
+    take = one_hot((iota((128, 128), 0) == group) & (iota((128, 128), 1) < 4))
+    cluster = jnp.dot(tag, take, preferred_element_type=jnp.float32)
+    marked = cluster == (iota(tag.shape, 1) + 1).astype(jnp.float32)
+    return jnp.where(marked, TAG, 0.0).astype(jnp.bfloat16)
 
 
 def spread(best, group):
@@ -94,7 +93,7 @@
 
 def own_kernel(groups_ref, tag_ref, a_ref, out_ref, marks_ref):
     tag = tag_ref[...]
-    for j in range(4):
+    for j in range(5):
         marks_ref[j * ROWS : (j + 1) * ROWS, :] = marks_of(tag, groups_ref[j])
     marks_a = marks_ref[:ROWS, :]
     a = a_ref[...]
@@ -107,22 +106,27 @@
     return marks_ref[j * ROWS : (j + 1) * ROWS, :]
 
 
-def previous_kernel(groups_ref, marks_ref, best_ref, a_ref, p_ref, out_ref):
-    marks_a, marks_p = marks(marks_ref, 0), marks(marks_ref, 2)
-    scores = nt_dot(a_ref[...], p_ref[...]) + nt_dot(marks_a, marks_p)
-    best = jnp.maximum(best_ref[...], spread(row_best(scores), groups_ref[0]))
-    out_ref[...] = jnp.maximum(best, spread(column_best(scores), groups_ref[2]))
-
-
-def last_kernel(groups_ref, marks_ref, best_ref, a_ref, b_ref, p_ref, n_ref, out_ref):
-    a, n = a_ref[...], n_ref[...]
-    marks_a, marks_n = marks(marks_ref, 0), marks(marks_ref, 3)
-    a_b = nt_dot(a, b_ref[...]) + nt_dot(marks_a, marks(marks_ref, 1))
-    a_n = nt_dot(a, n) + nt_dot(marks_a, marks_n)
-    p_n = nt_dot(p_ref[...], n) + nt_dot(marks(marks_ref, 2), marks_n)
-    best = jnp.maximum(best_ref[...], spread(row_best(jnp.maximum(a_n, a_b)), groups_ref[0]))
-    best = jnp.maximum(best, spread(row_best(p_n), groups_ref[2]))
-    out_ref[...] = jnp.maximum(best, spread(column_best(jnp.maximum(a_n, p_n)), groups_ref[3]))
+def with_marks(marks_ref, x, i, y, j):
+    return nt_dot(x, y) + nt_dot(marks(marks_ref, i), marks(marks_ref, j))
+
+
+def first_kernel(groups_ref, marks_ref, best_ref, a_ref, f_ref, b_ref, out_ref):
+    a = a_ref[...]
+    a_f = with_marks(marks_ref, a, 0, f_ref[...], 2)
+    a_b = with_marks(marks_ref, a, 0, b_ref[...], 1)
+    best = jnp.maximum(best_ref[...], spread(row_best(jnp.maximum(a_f, a_b)), groups_ref[0]))
+    out_ref[...] = jnp.maximum(best, spread(column_best(a_f), groups_ref[2]))
+
+
+def last_kernel(groups_ref, marks_ref, best_ref, a_ref, b_ref, f_ref, q_ref, s_ref, out_ref):
+    f, q, s = f_ref[...], q_ref[...], s_ref[...]
+    b_s = with_marks(marks_ref, b_ref[...], 1, s, 3)
+    f_s = with_marks(marks_ref, f, 2, s, 3)
+    a_q = with_marks(marks_ref, a_ref[...], 0, q, 4)
+    f_q = with_marks(marks_ref, f, 2, q, 4)
+    best = jnp.maximum(best_ref[...], spread(row_best(a_q), groups_ref[0]))
+    best = jnp.maximum(best, spread(row_best(b_s), groups_ref[1]))
+    out_ref[...] = jnp.maximum(best, spread(row_best(jnp.maximum(f_s, f_q)), groups_ref[2]))
 
 
 def pick_kernel(place_ref, best_ref, out_ref):
@@ -214,12 +218,14 @@
     rows, features = embeddings.shape
     tile = lax.axis_index("tile")
     chip, core = tile // 2, tile % 2
+    before, after = (chip + 3) % 4, (chip + 1) % 4
     groups = jnp.stack(
         [
             tile,
             2 * chip + 1 - core,
-            2 * ((chip + 3) % 4) + jnp.where(chip > 0, 1 - core, core),
-            2 * ((chip + 1) % 4) + jnp.where(chip == 3, 1 - core, core),
+            2 * jnp.where(core == 0, before, after) + core,
+            2 * jnp.where(core == 0, after, before) + core,
+            2 * jnp.where(core == 0, after, before) + 1 - core,
         ]
     ).astype(jnp.int32)
     packed, place = pack(tile, cluster_ids, padding, embeddings)
@@ -228,21 +234,17 @@
     received = received.reshape(ROWS, features + 128)
     a, tag = lax.optimization_barrier((received[:, :features], received[:, features:]))
     swap = [(2 * x + c, 2 * x + 1 - c) for x in range(4) for c in range(2)]
-    backward = [
-        (2 * ((x + 1) % 4) + c, 2 * x + (c ^ NEXT_CROSSED[x])) for x in range(4) for c in range(2)
-    ]
-    forward = [
-        (2 * ((x + 3) % 4) + c, 2 * x + (c ^ PREVIOUS_CROSSED[x]))
-        for x in range(4)
-        for c in range(2)
-    ]
-    p = lax.ppermute(a, "tile", forward)
-    n = lax.ppermute(a, "tile", backward)
+    up = [[(2 * x + c, 2 * ((x + 1) % 4) + c) for x in range(4)] for c in range(2)]
+    down = [[(2 * x + c, 2 * ((x + 3) % 4) + c) for x in range(4)] for c in range(2)]
+    first = lax.ppermute(a, "tile", up[0] + down[1])
     b = lax.ppermute(a, "tile", swap)
-    marks_shape = jax.ShapeDtypeStruct((4 * ROWS, 128), jnp.bfloat16)
+    marks_shape = jax.ShapeDtypeStruct((5 * ROWS, 128), jnp.bfloat16)
     best, marks = scores(own_kernel, groups, tag, a, out_shape=(PARTIAL, marks_shape))
-    best = scores(previous_kernel, groups, marks, best, a, p)
-    best = scores(last_kernel, groups, marks, best, a, b, p, n)
+    later, best = lax.optimization_barrier((a, best))
+    second = lax.ppermute(later, "tile", down[0] + up[1])
+    crossed = lax.ppermute(first, "tile", swap)
+    best = scores(first_kernel, groups, marks, best, a, first, b)
+    best = scores(last_kernel, groups, marks, best, a, b, first, crossed, second)
     best = jnp.broadcast_to(best.reshape(8, 1, 4, 128), (8, 2, 4, 128)).reshape(16, 4, 128)
     best = exchange(best, "zc").reshape(8, 2, 4, 128)
     best = jnp.max(best, axis=1)

time: 105 us -> 103 us (0.981)
  waiting for transfers between devices: 11.7 us -> 2.34 us
  starting transfers between devices: 11.5 us -> 19.9 us
  blocking collectives: 67.9 us -> 66.3 us
    ppermute x2 -> x3, waiting for transfers between devices: 11.7 us -> 2.34 us  [the longest x1 2.09 us: on_device(): second = lax.ppermute(later, 'tile', down[0] + up[1])]
    ppermute x2 -> x3, starting transfers between devices: 9.62 us -> 16 us  [the longest x1 8.5 us: on_device(): crossed = lax.ppermute(first, 'tile', swap)]
    ppermute x1, starting transfers between devices: 1.92 us -> 3.88 us  [on_device(): b = lax.ppermute(a, 'tile', swap)]
    all_to_all x2, blocking collectives: 26 us -> 24.4 us  [exchange(): lax.all_to_all(array, ('dp', 'tile'), split_axis=0, concat_axis=0, axis_i...]
  transfers between devices with their start and end apart: 3 -> 4, of which waited for: 2 -> 2; matrix products, arithmetic and copies ran while one was open for 0% -> 0% of each run, Pallas kernels for 3% -> 3%
where the time goes in v4:
time: 103 us
  blocking collectives  66.3 us (64%)
  starting transfers between devices  19.9 us (19%)
  Pallas kernels  12.6 us (12%)
  waiting for transfers between devices  2.34 us (2%)
    all_to_all x1, blocking collectives, on_device(): lax.all_to_all(packed, 'dp', split_axis=0, concat_axis=0, tiled=True)  41.9 us
    all_to_all x2, blocking collectives, exchange(): lax.all_to_all(array, ('dp', 'tile'), split_axis=0, concat_axis=0, axis_i...  24.4 us
    ppermute x1, starting transfers between devices, on_device(): crossed = lax.ppermute(first, 'tile', swap)  8.5 us
    pallas_call x3, Pallas kernels, scores(): return call(kernel, out_shape, specs, flops)(groups, *arrays)  6.35 us
    ppermute x1, starting transfers between devices, on_device(): first = lax.ppermute(a, 'tile', up[0] + down[1])  4.39 us
    ppermute x1, starting transfers between devices, on_device(): b = lax.ppermute(a, 'tile', swap)  3.88 us
    pallas_call x1, Pallas kernels, pack(): call(pack_kernel, jax.ShapeDtypeStruct((ROWS, features + 128), jnp.bfloat...  3.51 us
    ppermute x1, starting transfers between devices, on_device(): second = lax.ppermute(later, 'tile', down[0] + up[1])  3.12 us
  transfers between devices with their start and end apart: 4, of which 2 were waited for; matrix products, arithmetic and copies ran while one was open for 0% of the time, Pallas kernels for 3%

profile of v4, /device:TPU:1, one launch (start us, length us, event | category | flops | bytes accessed | tf_op | source)
XLA Modules:
  0.0 103.1 jit_solution(8072635508422166221)
XLA Ops:
  0.0 0.0 copy-start
  0.0 0.9 compare_select_fusion
  0.9 1.4 %shard_map.37 = (s32[1,4096]{1,0:T(1,128)S(1)}, s32[1,4096]{1,0:T(1,128)S(1)}, bf16[512,128]{1,0:T(8,128)(2,1)S(1)}) custom-call(s32[1]{0:T(128)} %bitcast.tile_ref, s32[1,4096]{1,0:T(1,128)S(1)} %bitcast.20), custom_call_target="tpu_custom_call" | custom-call | flops 2000000000 | bytes 1048576 | tf_op jit(solution)/shard_map/pallas_call | solution.py:174
  2.3 0.5 copy-done
  2.8 3.5 %shard_map.38 = bf16[512,896]{1,0:T(8,128)(2,1)S(1)} custom-call(s32[1,4096]{1,0:T(1,128)S(1)} %get-tuple-element.15.wanted_ref, bf16[512,128]{1,0:T(8,128)(2,1)S(1)} %get-tuple-element.16.tag_ref, bf16[4096,768]{1,0:T(8,128)(2,1)S(1)} %copy-done), custom_call_target="tpu_custom_call" | custom-call | flops 3221225472 | bytes 1048576 | tf_op jit(solution)/shard_map/pallas_call | solution.py:181
  6.3 41.9 %all_to_all.15 = bf16[64,8,896]{2,1,0:T(8,128)(2,1)S(1)} all-to-all(bf16[64,8,896]{2,1,0:T(8,128)(2,1)S(1)} %bitcast.17), channel_id=1, replica_groups=mesh['dp'=64,'tile'=8] {'dp'}, dimensions={0} | all-to-all | bytes 1835008 | tf_op jit(solution)/shard_map/all_to_all | solution.py:233
  48.3 0.1 slice.24.a_ref
  48.3 4.4 %collective-permute-start = (bf16[512,768]{1,0:T(8,128)(2,1)S(1)}, bf16[512,768]{1,0:T(8,128)(2,1)S(1)}, u32[]{:S(2)}, u32[]{:S(2)}) collective-permute-start(bf16[512,768]{1,0:T(8,128)(2,1)S(1)} %slice.24.a_ref), channel_id=1, source_target_pairs={{0,2},{2,4},{4,6},{6,0},{1,7},{3,1},{5,3},{7,5},{8,10},{10,12},{12... | collective-permute-start | bytes 2359304 | tf_op jit(solution)/shard_map/ppermute | solution.py:239
  52.8 0.1 stack.20.groups_ref
  52.9 3.9 %collective-permute-start.1 = (bf16[512,768]{1,0:T(8,128)(2,1)S(1)}, bf16[512,768]{1,0:T(8,128)(2,1)S(1)}, u32[]{:S(2)}, u32[]{:S(2)}) collective-permute-start(bf16[512,768]{1,0:T(8,128)(2,1)S(1)} %slice.24.a_ref), channel_id=1, source_target_pairs={{0,1},{1,0},{2,3},{3,2},{4,5},{5,4},{6,7},{7,6},{8,9},{9,8},{10,11... | collective-permute-start | bytes 2359304 | tf_op jit(solution)/shard_map/ppermute | solution.py:240
  56.8 1.5 %shard_map.39 = (f32[32,128]{1,0:T(8,128)S(1)}, bf16[2560,128]{1,0:T(8,128)(2,1)S(1)}) custom-call(s32[5]{0:T(128)S(1)} %stack.20.groups_ref, bf16[512,128]{1,0:T(8,128)(2,1)S(1)} %slice.25.tag_ref, bf16[512,768]{1,0:T(8,128)(2,1)S(1)} %slice.24.a_ref), custom_call_target="tpu_custom_call" | custom-call | flops 805306368 | bytes 1048576 | tf_op jit(solution)/shard_map/pallas_call | solution.py:193
  58.3 3.1 %collective-permute-start.3 = (bf16[512,768]{1,0:T(8,128)(2,1)S(1)}, bf16[512,768]{1,0:T(8,128)(2,1)S(1)}, u32[]{:S(2)}, u32[]{:S(2)}) collective-permute-start(bf16[512,768]{1,0:T(8,128)(2,1)S(1)} %slice.24.a_ref), channel_id=1, source_target_pairs={{0,6},{2,0},{4,2},{6,4},{1,3},{3,5},{5,7},{7,1},{8,14},{10,8},{12,... | collective-permute-start | bytes 2359304 | tf_op jit(solution)/shard_map/ppermute | solution.py:244
  61.4 0.2 collective-permute-done.f_ref
  61.6 8.5 %collective-permute-start.2 = (bf16[512,768]{1,0:T(8,128)(2,1)S(1)}, bf16[512,768]{1,0:T(8,128)(2,1)S(1)}, u32[]{:S(2)}, u32[]{:S(2)}) collective-permute-start(bf16[512,768]{1,0:T(8,128)(2,1)S(1)} %collective-permute-done.f_ref), channel_id=1, source_target_pairs={{0,1},{1,0},{2,3},{3,2},{4,5},{5,4},{6,7},{7,6},{8,9},{9,8},{10,11... | collective-permute-start | bytes 2359304 | tf_op jit(solution)/shard_map/ppermute | solution.py:245
  70.2 0.0 collective-permute-done.1.b_ref
  70.2 1.9 %shard_map.40.best_ref = f32[32,128]{1,0:T(8,128)S(1)} custom-call(s32[5]{0:T(128)S(1)} %stack.20.groups_ref, bf16[2560,128]{1,0:T(8,128)(2,1)S(1)} %get-tuple-element.19.marks_ref, f32[32,128]{1,0:T(8,128)S(1)} %get-tuple-element.21.best_ref, bf16[512,768]{1,0:T(8,128)(2,1)S(1)} %slice.24.a_ref, bf16[512,768]{1,0:T(8,128)(2,1)S(1)} %collective-permute-done.f_ref, ...), custom_call_target="tpu_custom_call" | custom-call | flops 805306368 | bytes 1048576 | tf_op jit(solution)/shard_map/pallas_call | solution.py:193
  72.0 2.1 %collective-permute-done.3.s_ref = bf16[512,768]{1,0:T(8,128)(2,1)S(1)} collective-permute-done((bf16[512,768]{1,0:T(8,128)(2,1)S(1)}, bf16[512,768]{1,0:T(8,128)(2,1)S(1)}, u32[]{:S(2)}, u32[]{:S(2)}) %collective-permute-start.3) | collective-permute-done | bytes 786464 | tf_op jit(solution)/shard_map/ppermute | solution.py:244
  74.1 0.0 collective-permute-done.2.q_ref
  74.1 3.0 %shard_map.41 = f32[32,128]{1,0:T(8,128)S(1)} custom-call(s32[5]{0:T(128)S(1)} %stack.20.groups_ref, bf16[2560,128]{1,0:T(8,128)(2,1)S(1)} %get-tuple-element.19.marks_ref, f32[32,128]{1,0:T(8,128)S(1)} %shard_map.40.best_ref, bf16[512,768]{1,0:T(8,128)(2,1)S(1)} %slice.24.a_ref, bf16[512,768]{1,0:T(8,128)(2,1)S(1)} %collective-permute-done.1.b_ref, ...), custom_call_target="tpu_custom_call" | custom-call | flops 805306368 | bytes 1048576 | tf_op jit(solution)/shard_map/pallas_call | solution.py:193
  77.1 11.7 %all_to_all.16 = f32[16,4,128]{2,1,0:T(4,128)S(1)} all-to-all(f32[16,4,128]{2,1,0:T(4,128)S(1)} %bitcast.24), channel_id=1, replica_groups={{0,1,64,65,128,129,192,193,256,257,320,321,384,385,448,449},{2,3,66,67,..., dimensions={0} | all-to-all | bytes 65536 | tf_op jit(solution)/shard_map/all_to_all | solution.py:212
  88.8 0.1 fusion.1
  88.9 0.1 pad_maximum_fusion
  89.0 12.7 %all_to_all.17 = f32[32,4,128]{2,1,0:T(4,128)S(1)} all-to-all(f32[32,4,128]{2,1,0:T(4,128)S(1)} %bitcast.23), channel_id=1, replica_groups={{0,2,4,6,8,10,12,14,16,18,20,22,24,26,28,30,32,34,36,38,40,42,44,46,48,..., dimensions={0} | all-to-all | bytes 131072 | tf_op jit(solution)/shard_map/all_to_all | solution.py:212
  101.7 1.4 %shard_map.42 = f32[1,4096]{1,0:T(1,128)} custom-call(s32[1,4096]{1,0:T(1,128)S(1)} %get-tuple-element.14.place_ref, f32[8,4,4,128]{3,2,1,0:T(4,128)S(1)} %bitcast.18), custom_call_target="tpu_custom_call" | custom-call | bytes 1048576 | tf_op jit(solution)/shard_map/pallas_call | solution.py:198
  (8 shorter events, 0.1 us)
Async XLA Ops:
  0.0 2.8 %copy-start = (bf16[4096,768]{1,0:T(8,128)(2,1)S(1)}, bf16[4096,768]{1,0:T(8,128)(2,1)}, u32[]{:S(2)}) copy-start(bf16[4096,768]{1,0:T(8,128)(2,1)} %emb_ref.1) | copy-start | bytes 18874372
  48.3 13.3 %collective-permute-start = (bf16[512,768]{1,0:T(8,128)(2,1)S(1)}, bf16[512,768]{1,0:T(8,128)(2,1)S(1)}, u32[]{:S(2)}, u32[]{:S(2)}) collective-permute-start(bf16[512,768]{1,0:T(8,128)(2,1)S(1)} %slice.24.a_ref), channel_id=1, source_target_pairs={{0,2},{2,4},{4,6},{6,0},{1,7},{3,1},{5,3},{7,5},{8,10},{10,12},{12... | collective-permute-start | bytes 2359304 | tf_op jit(solution)/shard_map/ppermute | solution.py:239
  52.9 17.3 %collective-permute-start.1 = (bf16[512,768]{1,0:T(8,128)(2,1)S(1)}, bf16[512,768]{1,0:T(8,128)(2,1)S(1)}, u32[]{:S(2)}, u32[]{:S(2)}) collective-permute-start(bf16[512,768]{1,0:T(8,128)(2,1)S(1)} %slice.24.a_ref), channel_id=1, source_target_pairs={{0,1},{1,0},{2,3},{3,2},{4,5},{5,4},{6,7},{7,6},{8,9},{9,8},{10,11... | collective-permute-start | bytes 2359304 | tf_op jit(solution)/shard_map/ppermute | solution.py:240
  58.3 15.9 %collective-permute-start.3 = (bf16[512,768]{1,0:T(8,128)(2,1)S(1)}, bf16[512,768]{1,0:T(8,128)(2,1)S(1)}, u32[]{:S(2)}, u32[]{:S(2)}) collective-permute-start(bf16[512,768]{1,0:T(8,128)(2,1)S(1)} %slice.24.a_ref), channel_id=1, source_target_pairs={{0,6},{2,0},{4,2},{6,4},{1,3},{3,5},{5,7},{7,1},{8,14},{10,8},{12,... | collective-permute-start | bytes 2359304 | tf_op jit(solution)/shard_map/ppermute | solution.py:244
  61.6 12.5 %collective-permute-start.2 = (bf16[512,768]{1,0:T(8,128)(2,1)S(1)}, bf16[512,768]{1,0:T(8,128)(2,1)S(1)}, u32[]{:S(2)}, u32[]{:S(2)}) collective-permute-start(bf16[512,768]{1,0:T(8,128)(2,1)S(1)} %collective-permute-done.f_ref), channel_id=1, source_target_pairs={{0,1},{1,0},{2,3},{3,2},{4,5},{5,4},{6,7},{7,6},{8,9},{9,8},{10,11... | collective-permute-start | bytes 2359304 | tf_op jit(solution)/shard_map/ppermute | solution.py:245

commit v5 on v4

--- a/solution.py
+++ b/solution.py
@@ -10,7 +10,7 @@
 TILES = 8
 PART = CAPACITY // TILES
 ROWS = OWNERS * PART
-TAG = 2.0
+PARTS = 5
 PLACE_FLOPS = 2_000_000_000
 VMEM = 16 * 1024 * 1024
 
@@ -66,18 +66,18 @@
     unit_ref[:, features:] = tag_ref[...]
 
 
-def marks_of(tag, group):
-    take = one_hot((iota((128, 128), 0) == group) & (iota((128, 128), 1) < 4))
-    cluster = jnp.dot(tag, take, preferred_element_type=jnp.float32)
-    marked = cluster == (iota(tag.shape, 1) + 1).astype(jnp.float32)
-    return jnp.where(marked, TAG, 0.0).astype(jnp.bfloat16)
-
-
-def spread(best, group):
+def clusters_of(tag, group):
+    take = one_hot(iota((128, 128), 0) == group)
+    return jnp.dot(tag, take, preferred_element_type=jnp.float32)
+
+
+def spread(*bests):
     row, lane = iota((ROWS, 128), 0), iota((ROWS, 128), 1)
-    value = jnp.maximum(best - TAG * TAG, -1.0)
-    here = lane == group * PART + (row & 7) + ((row >> 5) & 1) * CAPACITY
-    placed = jnp.where(here, value, -2.0).reshape(8, 2, 4, PART, 128)
+    slot = lane - (row & 7) - ((row >> 5) & 1) * CAPACITY
+    placed = jnp.full((ROWS, 128), -2.0, jnp.float32)
+    for best, group in bests:
+        placed = jnp.where(slot == group * PART, jnp.maximum(best, -1.0), placed)
+    placed = placed.reshape(8, 2, 4, PART, 128)
     return jnp.max(jnp.max(placed, axis=1), axis=2).reshape(32, 128)
 
 
@@ -91,42 +91,49 @@
     return jnp.broadcast_to(best, (128, ROWS)).T[:, :1]
 
 
-def own_kernel(groups_ref, tag_ref, a_ref, out_ref, marks_ref):
+def same_cluster(rows_ref, i, columns_ref, j):
+    rows = rows_ref[i * ROWS : (i + 1) * ROWS, :]
+    return jnp.concatenate([rows] * (ROWS // 128), axis=1) == columns_ref[j * 8 : j * 8 + 1, :]
+
+
+def masked_scores(rows_ref, columns_ref, x, i, y, j):
+    return jnp.where(same_cluster(rows_ref, i, columns_ref, j), nt_dot(x, y), -1.0)
+
+
+def own_kernel(groups_ref, tag_ref, a_ref, out_ref, rows_ref, columns_ref):
     tag = tag_ref[...]
-    for j in range(5):
-        marks_ref[j * ROWS : (j + 1) * ROWS, :] = marks_of(tag, groups_ref[j])
-    marks_a = marks_ref[:ROWS, :]
+    for j in range(PARTS):
+        clusters = clusters_of(tag, groups_ref[j])
+        rows_ref[j * ROWS : (j + 1) * ROWS, :] = jnp.where(clusters == 0.0, -1.0, clusters)
+        columns_ref[j * 8 : (j + 1) * 8, :] = clusters.T[:8, :]
     a = a_ref[...]
-    same = nt_dot(a, a) + nt_dot(marks_a, marks_a)
-    same = jnp.where(iota((ROWS, ROWS), 0) == iota((ROWS, ROWS), 1), -2.0, same)
-    out_ref[...] = spread(row_best(same), groups_ref[0])
-
-
-def marks(marks_ref, j):
-    return marks_ref[j * ROWS : (j + 1) * ROWS, :]
-
-
-def with_marks(marks_ref, x, i, y, j):
-    return nt_dot(x, y) + nt_dot(marks(marks_ref, i), marks(marks_ref, j))
-
-
-def first_kernel(groups_ref, marks_ref, best_ref, a_ref, f_ref, b_ref, out_ref):
+    scores = masked_scores(rows_ref, columns_ref, a, 0, a, 0)
+    scores = jnp.where(iota((ROWS, ROWS), 0) == iota((ROWS, ROWS), 1), -1.0, scores)
+    out_ref[...] = spread((row_best(scores), groups_ref[0]))
+
+
+def first_kernel(groups_ref, rows_ref, columns_ref, best_ref, a_ref, f_ref, b_ref, out_ref):
     a = a_ref[...]
-    a_f = with_marks(marks_ref, a, 0, f_ref[...], 2)
-    a_b = with_marks(marks_ref, a, 0, b_ref[...], 1)
-    best = jnp.maximum(best_ref[...], spread(row_best(jnp.maximum(a_f, a_b)), groups_ref[0]))
-    out_ref[...] = jnp.maximum(best, spread(column_best(a_f), groups_ref[2]))
-
-
-def last_kernel(groups_ref, marks_ref, best_ref, a_ref, b_ref, f_ref, q_ref, s_ref, out_ref):
+    a_f = masked_scores(rows_ref, columns_ref, a, 0, f_ref[...], 2)
+    a_b = masked_scores(rows_ref, columns_ref, a, 0, b_ref[...], 1)
+    best = spread(
+        (row_best(jnp.maximum(a_f, a_b)), groups_ref[0]), (column_best(a_f), groups_ref[2])
+    )
+    out_ref[...] = jnp.maximum(best_ref[...], best)
+
+
+def last_kernel(groups_ref, rows_ref, columns_ref, best_ref, a_ref, b_ref, f_ref, q_ref, s_ref, out_ref):
     f, q, s = f_ref[...], q_ref[...], s_ref[...]
-    b_s = with_marks(marks_ref, b_ref[...], 1, s, 3)
-    f_s = with_marks(marks_ref, f, 2, s, 3)
-    a_q = with_marks(marks_ref, a_ref[...], 0, q, 4)
-    f_q = with_marks(marks_ref, f, 2, q, 4)
-    best = jnp.maximum(best_ref[...], spread(row_best(a_q), groups_ref[0]))
-    best = jnp.maximum(best, spread(row_best(b_s), groups_ref[1]))
-    out_ref[...] = jnp.maximum(best, spread(row_best(jnp.maximum(f_s, f_q)), groups_ref[2]))
+    b_s = masked_scores(rows_ref, columns_ref, b_ref[...], 1, s, 3)
+    f_s = masked_scores(rows_ref, columns_ref, f, 2, s, 3)
+    a_q = masked_scores(rows_ref, columns_ref, a_ref[...], 0, q, 4)
+    f_q = masked_scores(rows_ref, columns_ref, f, 2, q, 4)
+    best = spread(
+        (row_best(a_q), groups_ref[0]),
+        (row_best(b_s), groups_ref[1]),
+        (row_best(jnp.maximum(f_s, f_q)), groups_ref[2]),
+    )
+    out_ref[...] = jnp.maximum(best_ref[...], best)
 
 
 def pick_kernel(place_ref, best_ref, out_ref):
@@ -238,13 +245,16 @@
     down = [[(2 * x + c, 2 * ((x + 3) % 4) + c) for x in range(4)] for c in range(2)]
     first = lax.ppermute(a, "tile", up[0] + down[1])
     b = lax.ppermute(a, "tile", swap)
-    marks_shape = jax.ShapeDtypeStruct((5 * ROWS, 128), jnp.bfloat16)
-    best, marks = scores(own_kernel, groups, tag, a, out_shape=(PARTIAL, marks_shape))
+    clusters = [
+        jax.ShapeDtypeStruct((PARTS * ROWS, 128), jnp.float32),
+        jax.ShapeDtypeStruct((PARTS * 8, ROWS), jnp.float32),
+    ]
+    best, *clusters = scores(own_kernel, groups, tag, a, out_shape=[PARTIAL] + clusters)
     later, best = lax.optimization_barrier((a, best))
     second = lax.ppermute(later, "tile", down[0] + up[1])
     crossed = lax.ppermute(first, "tile", swap)
-    best = scores(first_kernel, groups, marks, best, a, first, b)
-    best = scores(last_kernel, groups, marks, best, a, b, first, crossed, second)
+    best = scores(first_kernel, groups, *clusters, best, a, first, b)
+    best = scores(last_kernel, groups, *clusters, best, a, b, first, crossed, second)
     best = jnp.broadcast_to(best.reshape(8, 1, 4, 128), (8, 2, 4, 128)).reshape(16, 4, 128)
     best = exchange(best, "zc").reshape(8, 2, 4, 128)
     best = jnp.max(best, axis=1)

time: 103 us -> 103 us (level)
  no operation moved by 1% of the time
where the time goes in v5:
time: 103 us
  blocking collectives  66.3 us (64%)
  starting transfers between devices  20 us (19%)
  Pallas kernels  12 us (12%)
  waiting for transfers between devices  2.51 us (2%)
    all_to_all x1, blocking collectives, on_device(): lax.all_to_all(packed, 'dp', split_axis=0, concat_axis=0, tiled=True)  41.9 us
    all_to_all x2, blocking collectives, exchange(): lax.all_to_all(array, ('dp', 'tile'), split_axis=0, concat_axis=0, axis_i...  24.4 us
    ppermute x1, starting transfers between devices, on_device(): crossed = lax.ppermute(first, 'tile', swap)  8.61 us
    pallas_call x3, Pallas kernels, scores(): return call(kernel, out_shape, specs, flops)(groups, *arrays)  5.67 us
    ppermute x1, starting transfers between devices, on_device(): first = lax.ppermute(a, 'tile', up[0] + down[1])  4.39 us
    ppermute x1, starting transfers between devices, on_device(): b = lax.ppermute(a, 'tile', swap)  3.88 us
    pallas_call x1, Pallas kernels, pack(): call(pack_kernel, jax.ShapeDtypeStruct((ROWS, features + 128), jnp.bfloat...  3.51 us
    ppermute x1, starting transfers between devices, on_device(): second = lax.ppermute(later, 'tile', down[0] + up[1])  3.12 us
  transfers between devices with their start and end apart: 4, of which 2 were waited for; matrix products, arithmetic and copies ran while one was open for 0% of the time, Pallas kernels for 3%

profile of v5, /device:TPU:1, one launch (start us, length us, event | category | flops | bytes accessed | tf_op | source)
XLA Modules:
  0.0 102.7 jit_solution(9911905497202795232)
XLA Ops:
  0.0 0.0 copy-start
  0.0 0.9 compare_select_fusion
  0.9 1.4 %shard_map.37 = (s32[1,4096]{1,0:T(1,128)S(1)}, s32[1,4096]{1,0:T(1,128)S(1)}, bf16[512,128]{1,0:T(8,128)(2,1)S(1)}) custom-call(s32[1]{0:T(128)} %bitcast.tile_ref, s32[1,4096]{1,0:T(1,128)S(1)} %bitcast.20), custom_call_target="tpu_custom_call" | custom-call | flops 2000000000 | bytes 1048576 | tf_op jit(solution)/shard_map/pallas_call | solution.py:181
  2.3 0.5 copy-done
  2.8 3.5 %shard_map.38 = bf16[512,896]{1,0:T(8,128)(2,1)S(1)} custom-call(s32[1,4096]{1,0:T(1,128)S(1)} %get-tuple-element.16.wanted_ref, bf16[512,128]{1,0:T(8,128)(2,1)S(1)} %get-tuple-element.17.tag_ref, bf16[4096,768]{1,0:T(8,128)(2,1)S(1)} %copy-done), custom_call_target="tpu_custom_call" | custom-call | flops 3221225472 | bytes 1048576 | tf_op jit(solution)/shard_map/pallas_call | solution.py:188
  6.3 41.9 %all_to_all.15 = bf16[64,8,896]{2,1,0:T(8,128)(2,1)S(1)} all-to-all(bf16[64,8,896]{2,1,0:T(8,128)(2,1)S(1)} %bitcast.17), channel_id=1, replica_groups=mesh['dp'=64,'tile'=8] {'dp'}, dimensions={0} | all-to-all | bytes 1835008 | tf_op jit(solution)/shard_map/all_to_all | solution.py:240
  48.3 0.1 slice.24.a_ref
  48.3 4.4 %collective-permute-start = (bf16[512,768]{1,0:T(8,128)(2,1)S(1)}, bf16[512,768]{1,0:T(8,128)(2,1)S(1)}, u32[]{:S(2)}, u32[]{:S(2)}) collective-permute-start(bf16[512,768]{1,0:T(8,128)(2,1)S(1)} %slice.24.a_ref), channel_id=1, source_target_pairs={{0,2},{2,4},{4,6},{6,0},{1,7},{3,1},{5,3},{7,5},{8,10},{10,12},{12... | collective-permute-start | bytes 2359304 | tf_op jit(solution)/shard_map/ppermute | solution.py:246
  52.8 0.1 stack.20.groups_ref
  52.9 3.9 %collective-permute-start.1 = (bf16[512,768]{1,0:T(8,128)(2,1)S(1)}, bf16[512,768]{1,0:T(8,128)(2,1)S(1)}, u32[]{:S(2)}, u32[]{:S(2)}) collective-permute-start(bf16[512,768]{1,0:T(8,128)(2,1)S(1)} %slice.24.a_ref), channel_id=1, source_target_pairs={{0,1},{1,0},{2,3},{3,2},{4,5},{5,4},{6,7},{7,6},{8,9},{9,8},{10,11... | collective-permute-start | bytes 2359304 | tf_op jit(solution)/shard_map/ppermute | solution.py:247
  56.8 1.4 %shard_map.39 = (f32[32,128]{1,0:T(8,128)S(1)}, f32[2560,128]{1,0:T(8,128)S(1)}, f32[40,512]{1,0:T(8,128)S(1)}) custom-call(s32[5]{0:T(128)S(1)} %stack.20.groups_ref, bf16[512,128]{1,0:T(8,128)(2,1)S(1)} %slice.25.tag_ref, bf16[512,768]{1,0:T(8,128)(2,1)S(1)} %slice.24.a_ref), custom_call_target="tpu_custom_call" | custom-call | flops 805306368 | bytes 1048576 | tf_op jit(solution)/shard_map/pallas_call | solution.py:200
  58.2 3.1 %collective-permute-start.3 = (bf16[512,768]{1,0:T(8,128)(2,1)S(1)}, bf16[512,768]{1,0:T(8,128)(2,1)S(1)}, u32[]{:S(2)}, u32[]{:S(2)}) collective-permute-start(bf16[512,768]{1,0:T(8,128)(2,1)S(1)} %slice.24.a_ref), channel_id=1, source_target_pairs={{0,6},{2,0},{4,2},{6,4},{1,3},{3,5},{5,7},{7,1},{8,14},{10,8},{12,... | collective-permute-start | bytes 2359304 | tf_op jit(solution)/shard_map/ppermute | solution.py:254
  61.3 0.4 collective-permute-done.f_ref
  61.6 8.6 %collective-permute-start.2 = (bf16[512,768]{1,0:T(8,128)(2,1)S(1)}, bf16[512,768]{1,0:T(8,128)(2,1)S(1)}, u32[]{:S(2)}, u32[]{:S(2)}) collective-permute-start(bf16[512,768]{1,0:T(8,128)(2,1)S(1)} %collective-permute-done.f_ref), channel_id=1, source_target_pairs={{0,1},{1,0},{2,3},{3,2},{4,5},{5,4},{6,7},{7,6},{8,9},{9,8},{10,11... | collective-permute-start | bytes 2359304 | tf_op jit(solution)/shard_map/ppermute | solution.py:255
  70.3 0.0 collective-permute-done.1.b_ref
  70.3 1.7 %shard_map.40.best_ref = f32[32,128]{1,0:T(8,128)S(1)} custom-call(s32[5]{0:T(128)S(1)} %stack.20.groups_ref, f32[2560,128]{1,0:T(8,128)S(1)} %get-tuple-element.20.rows_ref, f32[40,512]{1,0:T(8,128)S(1)} %get-tuple-element.21.columns_ref, f32[32,128]{1,0:T(8,128)S(1)} %get-tuple-element.23.best_ref, bf16[512,768]{1,0:T(8,128)(2,1)S(1)} %slice.24.a_ref, ...), custom_call_target="tpu_custom_call" | custom-call | flops 805306368 | bytes 1048576 | tf_op jit(solution)/shard_map/pallas_call | solution.py:200
  72.0 2.1 %collective-permute-done.3.s_ref = bf16[512,768]{1,0:T(8,128)(2,1)S(1)} collective-permute-done((bf16[512,768]{1,0:T(8,128)(2,1)S(1)}, bf16[512,768]{1,0:T(8,128)(2,1)S(1)}, u32[]{:S(2)}, u32[]{:S(2)}) %collective-permute-start.3) | collective-permute-done | bytes 786464 | tf_op jit(solution)/shard_map/ppermute | solution.py:254
  74.1 0.0 collective-permute-done.2.q_ref
  74.1 2.6 %shard_map.41 = f32[32,128]{1,0:T(8,128)S(1)} custom-call(s32[5]{0:T(128)S(1)} %stack.20.groups_ref, f32[2560,128]{1,0:T(8,128)S(1)} %get-tuple-element.20.rows_ref, f32[40,512]{1,0:T(8,128)S(1)} %get-tuple-element.21.columns_ref, f32[32,128]{1,0:T(8,128)S(1)} %shard_map.40.best_ref, bf16[512,768]{1,0:T(8,128)(2,1)S(1)} %slice.24.a_ref, ...), custom_call_target="tpu_custom_call" | custom-call | flops 805306368 | bytes 1048576 | tf_op jit(solution)/shard_map/pallas_call | solution.py:200
  76.7 11.7 %all_to_all.16 = f32[16,4,128]{2,1,0:T(4,128)S(1)} all-to-all(f32[16,4,128]{2,1,0:T(4,128)S(1)} %bitcast.24), channel_id=1, replica_groups={{0,1,64,65,128,129,192,193,256,257,320,321,384,385,448,449},{2,3,66,67,..., dimensions={0} | all-to-all | bytes 65536 | tf_op jit(solution)/shard_map/all_to_all | solution.py:219
  88.4 0.1 fusion.1
  88.5 0.1 pad_maximum_fusion
  88.6 12.7 %all_to_all.17 = f32[32,4,128]{2,1,0:T(4,128)S(1)} all-to-all(f32[32,4,128]{2,1,0:T(4,128)S(1)} %bitcast.23), channel_id=1, replica_groups={{0,2,4,6,8,10,12,14,16,18,20,22,24,26,28,30,32,34,36,38,40,42,44,46,48,..., dimensions={0} | all-to-all | bytes 131072 | tf_op jit(solution)/shard_map/all_to_all | solution.py:219
  101.3 1.4 %shard_map.42 = f32[1,4096]{1,0:T(1,128)} custom-call(s32[1,4096]{1,0:T(1,128)S(1)} %get-tuple-element.15.place_ref, f32[8,4,4,128]{3,2,1,0:T(4,128)S(1)} %bitcast.18), custom_call_target="tpu_custom_call" | custom-call | bytes 1048576 | tf_op jit(solution)/shard_map/pallas_call | solution.py:205
  (8 shorter events, 0.1 us)
Async XLA Ops:
  0.0 2.8 %copy-start = (bf16[4096,768]{1,0:T(8,128)(2,1)S(1)}, bf16[4096,768]{1,0:T(8,128)(2,1)}, u32[]{:S(2)}) copy-start(bf16[4096,768]{1,0:T(8,128)(2,1)} %emb_ref.1) | copy-start | bytes 18874372
  48.3 13.3 %collective-permute-start = (bf16[512,768]{1,0:T(8,128)(2,1)S(1)}, bf16[512,768]{1,0:T(8,128)(2,1)S(1)}, u32[]{:S(2)}, u32[]{:S(2)}) collective-permute-start(bf16[512,768]{1,0:T(8,128)(2,1)S(1)} %slice.24.a_ref), channel_id=1, source_target_pairs={{0,2},{2,4},{4,6},{6,0},{1,7},{3,1},{5,3},{7,5},{8,10},{10,12},{12... | collective-permute-start | bytes 2359304 | tf_op jit(solution)/shard_map/ppermute | solution.py:246
  52.9 17.4 %collective-permute-start.1 = (bf16[512,768]{1,0:T(8,128)(2,1)S(1)}, bf16[512,768]{1,0:T(8,128)(2,1)S(1)}, u32[]{:S(2)}, u32[]{:S(2)}) collective-permute-start(bf16[512,768]{1,0:T(8,128)(2,1)S(1)} %slice.24.a_ref), channel_id=1, source_target_pairs={{0,1},{1,0},{2,3},{3,2},{4,5},{5,4},{6,7},{7,6},{8,9},{9,8},{10,11... | collective-permute-start | bytes 2359304 | tf_op jit(solution)/shard_map/ppermute | solution.py:247
  58.2 16.0 %collective-permute-start.3 = (bf16[512,768]{1,0:T(8,128)(2,1)S(1)}, bf16[512,768]{1,0:T(8,128)(2,1)S(1)}, u32[]{:S(2)}, u32[]{:S(2)}) collective-permute-start(bf16[512,768]{1,0:T(8,128)(2,1)S(1)} %slice.24.a_ref), channel_id=1, source_target_pairs={{0,6},{2,0},{4,2},{6,4},{1,3},{3,5},{5,7},{7,1},{8,14},{10,8},{12,... | collective-permute-start | bytes 2359304 | tf_op jit(solution)/shard_map/ppermute | solution.py:254
  61.6 12.5 %collective-permute-start.2 = (bf16[512,768]{1,0:T(8,128)(2,1)S(1)}, bf16[512,768]{1,0:T(8,128)(2,1)S(1)}, u32[]{:S(2)}, u32[]{:S(2)}) collective-permute-start(bf16[512,768]{1,0:T(8,128)(2,1)S(1)} %collective-permute-done.f_ref), channel_id=1, source_target_pairs={{0,1},{1,0},{2,3},{3,2},{4,5},{5,4},{6,7},{7,6},{8,9},{9,8},{10,11... | collective-permute-start | bytes 2359304 | tf_op jit(solution)/shard_map/ppermute | solution.py:255

commit v6 on v5

--- a/solution.py
+++ b/solution.py
@@ -142,7 +142,7 @@
     owner = place >> 6
     z, y = owner >> 3, owner & 7
     owner_hot = one_hot(((z >> 2) << 5) + (y << 2) + (z & 3) == iota((OWNERS, rows), 0))
-    best = jnp.max(best_ref[...], axis=1).reshape(32, 128).T
+    best = jnp.max(best_ref[...], axis=0).reshape(32, 128).T
     best = jnp.concatenate([best[:CAPACITY], best[CAPACITY:]], axis=1)
     high = best.astype(jnp.bfloat16)
     rest = best - high.astype(jnp.float32)
@@ -209,12 +209,11 @@
     sizes = dict(z=8, y=8, x=4, c=2)
     strides = dict(z=64, y=8, x=2, c=1)
     members, starts = [0], [0]
-    for axis in "zyxc":
-        steps = [i * strides[axis] for i in range(sizes[axis])]
-        if axis in axes:
-            members = [m + i for m in members for i in steps]
-        else:
-            starts = [m + i for m in starts for i in steps]
+    for axis in axes:
+        members = [m + i * strides[axis] for m in members for i in range(sizes[axis])]
+    for axis in sizes:
+        if axis not in axes:
+            starts = [m + i * strides[axis] for m in starts for i in range(sizes[axis])]
     groups = [[start + m for m in members] for start in starts]
     return lax.all_to_all(
         array, ("dp", "tile"), split_axis=0, concat_axis=0, axis_index_groups=groups, tiled=True
@@ -255,14 +254,14 @@
     crossed = lax.ppermute(first, "tile", swap)
     best = scores(first_kernel, groups, *clusters, best, a, first, b)
     best = scores(last_kernel, groups, *clusters, best, a, b, first, crossed, second)
-    best = jnp.broadcast_to(best.reshape(8, 1, 4, 128), (8, 2, 4, 128)).reshape(16, 4, 128)
-    best = exchange(best, "zc").reshape(8, 2, 4, 128)
-    best = jnp.max(best, axis=1)
+    best = jnp.broadcast_to(best.reshape(1, 8, 4, 128), (2, 8, 4, 128)).reshape(16, 4, 128)
+    best = exchange(best, "cz").reshape(2, 8, 4, 128)
+    best = jnp.max(best, axis=0)
     best = jnp.concatenate([best[:, :, :CAPACITY], best[:, :, CAPACITY:]], axis=1)
     best = best.transpose(1, 0, 2)
     best = jnp.concatenate([best[:, :4], best[:, 4:]], axis=2)
-    best = jnp.broadcast_to(best[:, None], (8, 4, 4, 128)).reshape(32, 4, 128)
-    best = exchange(best, "yx").reshape(8, 4, 4, 128)
+    best = jnp.broadcast_to(best[None], (4, 8, 4, 128)).reshape(32, 4, 128)
+    best = exchange(best, "xy").reshape(4, 8, 4, 128)
     return pick(place, best).reshape(rows)
 
 

time: 103 us -> 103 us (level)
  no operation moved by 1% of the time
where the time goes in v6:
time: 103 us; the launch traced here: 102 us
  blocking collectives  66 us (64%)
  starting transfers between devices  20 us (19%)
  Pallas kernels  12 us (12%)
  waiting for transfers between devices  2.51 us (2%)
    all_to_all x1, blocking collectives, on_device(): lax.all_to_all(packed, 'dp', split_axis=0, concat_axis=0, tiled=True)  41.9 us
    all_to_all x2, blocking collectives, exchange(): lax.all_to_all(array, ('dp', 'tile'), split_axis=0, concat_axis=0, axis_i...  24.1 us
    ppermute x1, starting transfers between devices, on_device(): crossed = lax.ppermute(first, 'tile', swap)  8.61 us
    pallas_call x3, Pallas kernels, scores(): return call(kernel, out_shape, specs, flops)(groups, *arrays)  5.67 us
    ppermute x1, starting transfers between devices, on_device(): first = lax.ppermute(a, 'tile', up[0] + down[1])  4.39 us
    ppermute x1, starting transfers between devices, on_device(): b = lax.ppermute(a, 'tile', swap)  3.88 us
    pallas_call x1, Pallas kernels, pack(): call(pack_kernel, jax.ShapeDtypeStruct((ROWS, features + 128), jnp.bfloat...  3.51 us
    ppermute x1, starting transfers between devices, on_device(): second = lax.ppermute(later, 'tile', down[0] + up[1])  3.12 us
  transfers between devices with their start and end apart: 4, of which 2 were waited for; matrix products, arithmetic and copies ran while one was open for 0% of the time, Pallas kernels for 3%

profile of v6, /device:TPU:1, one launch (start us, length us, event | category | flops | bytes accessed | tf_op | source)
XLA Modules:
  0.0 102.4 jit_solution(4200400491343070730)
XLA Ops:
  0.0 0.0 copy-start
  0.0 0.9 compare_select_fusion
  0.9 1.4 %shard_map.37 = (s32[1,4096]{1,0:T(1,128)S(1)}, s32[1,4096]{1,0:T(1,128)S(1)}, bf16[512,128]{1,0:T(8,128)(2,1)S(1)}) custom-call(s32[1]{0:T(128)} %bitcast.tile_ref, s32[1,4096]{1,0:T(1,128)S(1)} %bitcast.19), custom_call_target="tpu_custom_call" | custom-call | flops 2000000000 | bytes 1048576 | tf_op jit(solution)/shard_map/pallas_call | solution.py:181
  2.3 0.5 copy-done
  2.8 3.5 %shard_map.38 = bf16[512,896]{1,0:T(8,128)(2,1)S(1)} custom-call(s32[1,4096]{1,0:T(1,128)S(1)} %get-tuple-element.16.wanted_ref, bf16[512,128]{1,0:T(8,128)(2,1)S(1)} %get-tuple-element.17.tag_ref, bf16[4096,768]{1,0:T(8,128)(2,1)S(1)} %copy-done), custom_call_target="tpu_custom_call" | custom-call | flops 3221225472 | bytes 1048576 | tf_op jit(solution)/shard_map/pallas_call | solution.py:188
  6.3 41.9 %all_to_all.15 = bf16[64,8,896]{2,1,0:T(8,128)(2,1)S(1)} all-to-all(bf16[64,8,896]{2,1,0:T(8,128)(2,1)S(1)} %bitcast.16), channel_id=1, replica_groups=mesh['dp'=64,'tile'=8] {'dp'}, dimensions={0} | all-to-all | bytes 1835008 | tf_op jit(solution)/shard_map/all_to_all | solution.py:239
  48.3 0.1 slice.24.a_ref
  48.3 4.4 %collective-permute-start = (bf16[512,768]{1,0:T(8,128)(2,1)S(1)}, bf16[512,768]{1,0:T(8,128)(2,1)S(1)}, u32[]{:S(2)}, u32[]{:S(2)}) collective-permute-start(bf16[512,768]{1,0:T(8,128)(2,1)S(1)} %slice.24.a_ref), channel_id=1, source_target_pairs={{0,2},{2,4},{4,6},{6,0},{1,7},{3,1},{5,3},{7,5},{8,10},{10,12},{12... | collective-permute-start | bytes 2359304 | tf_op jit(solution)/shard_map/ppermute | solution.py:245
  52.8 0.1 stack.20.groups_ref
  52.9 3.9 %collective-permute-start.1 = (bf16[512,768]{1,0:T(8,128)(2,1)S(1)}, bf16[512,768]{1,0:T(8,128)(2,1)S(1)}, u32[]{:S(2)}, u32[]{:S(2)}) collective-permute-start(bf16[512,768]{1,0:T(8,128)(2,1)S(1)} %slice.24.a_ref), channel_id=1, source_target_pairs={{0,1},{1,0},{2,3},{3,2},{4,5},{5,4},{6,7},{7,6},{8,9},{9,8},{10,11... | collective-permute-start | bytes 2359304 | tf_op jit(solution)/shard_map/ppermute | solution.py:246
  56.8 1.4 %shard_map.39 = (f32[32,128]{1,0:T(8,128)S(1)}, f32[2560,128]{1,0:T(8,128)S(1)}, f32[40,512]{1,0:T(8,128)S(1)}) custom-call(s32[5]{0:T(128)S(1)} %stack.20.groups_ref, bf16[512,128]{1,0:T(8,128)(2,1)S(1)} %slice.25.tag_ref, bf16[512,768]{1,0:T(8,128)(2,1)S(1)} %slice.24.a_ref), custom_call_target="tpu_custom_call" | custom-call | flops 805306368 | bytes 1048576 | tf_op jit(solution)/shard_map/pallas_call | solution.py:200
  58.2 3.1 %collective-permute-start.3 = (bf16[512,768]{1,0:T(8,128)(2,1)S(1)}, bf16[512,768]{1,0:T(8,128)(2,1)S(1)}, u32[]{:S(2)}, u32[]{:S(2)}) collective-permute-start(bf16[512,768]{1,0:T(8,128)(2,1)S(1)} %slice.24.a_ref), channel_id=1, source_target_pairs={{0,6},{2,0},{4,2},{6,4},{1,3},{3,5},{5,7},{7,1},{8,14},{10,8},{12,... | collective-permute-start | bytes 2359304 | tf_op jit(solution)/shard_map/ppermute | solution.py:253
  61.3 0.4 collective-permute-done.f_ref
  61.6 8.6 %collective-permute-start.2 = (bf16[512,768]{1,0:T(8,128)(2,1)S(1)}, bf16[512,768]{1,0:T(8,128)(2,1)S(1)}, u32[]{:S(2)}, u32[]{:S(2)}) collective-permute-start(bf16[512,768]{1,0:T(8,128)(2,1)S(1)} %collective-permute-done.f_ref), channel_id=1, source_target_pairs={{0,1},{1,0},{2,3},{3,2},{4,5},{5,4},{6,7},{7,6},{8,9},{9,8},{10,11... | collective-permute-start | bytes 2359304 | tf_op jit(solution)/shard_map/ppermute | solution.py:254
  70.3 0.0 collective-permute-done.1.b_ref
  70.3 1.7 %shard_map.40.best_ref = f32[32,128]{1,0:T(8,128)S(1)} custom-call(s32[5]{0:T(128)S(1)} %stack.20.groups_ref, f32[2560,128]{1,0:T(8,128)S(1)} %get-tuple-element.20.rows_ref, f32[40,512]{1,0:T(8,128)S(1)} %get-tuple-element.21.columns_ref, f32[32,128]{1,0:T(8,128)S(1)} %get-tuple-element.23.best_ref, bf16[512,768]{1,0:T(8,128)(2,1)S(1)} %slice.24.a_ref, ...), custom_call_target="tpu_custom_call" | custom-call | flops 805306368 | bytes 1048576 | tf_op jit(solution)/shard_map/pallas_call | solution.py:200
  72.0 2.1 %collective-permute-done.3.s_ref = bf16[512,768]{1,0:T(8,128)(2,1)S(1)} collective-permute-done((bf16[512,768]{1,0:T(8,128)(2,1)S(1)}, bf16[512,768]{1,0:T(8,128)(2,1)S(1)}, u32[]{:S(2)}, u32[]{:S(2)}) %collective-permute-start.3) | collective-permute-done | bytes 786464 | tf_op jit(solution)/shard_map/ppermute | solution.py:253
  74.1 0.0 collective-permute-done.2.q_ref
  74.1 2.6 %shard_map.41 = f32[32,128]{1,0:T(8,128)S(1)} custom-call(s32[5]{0:T(128)S(1)} %stack.20.groups_ref, f32[2560,128]{1,0:T(8,128)S(1)} %get-tuple-element.20.rows_ref, f32[40,512]{1,0:T(8,128)S(1)} %get-tuple-element.21.columns_ref, f32[32,128]{1,0:T(8,128)S(1)} %shard_map.40.best_ref, bf16[512,768]{1,0:T(8,128)(2,1)S(1)} %slice.24.a_ref, ...), custom_call_target="tpu_custom_call" | custom-call | flops 805306368 | bytes 1048576 | tf_op jit(solution)/shard_map/pallas_call | solution.py:200
  76.7 11.3 %all_to_all.16 = f32[16,4,128]{2,1,0:T(4,128)S(1)} all-to-all(f32[16,4,128]{2,1,0:T(4,128)S(1)} %bitcast.24), channel_id=1, replica_groups={{0,64,128,192,256,320,384,448,1,65,129,193,257,321,385,449},{2,66,130,1..., dimensions={0} | all-to-all | bytes 65536 | tf_op jit(solution)/shard_map/all_to_all | solution.py:218
  88.1 0.1 fusion.1
  88.2 0.1 pad_maximum_fusion
  88.3 12.7 %all_to_all.17 = f32[32,4,128]{2,1,0:T(4,128)S(1)} all-to-all(f32[32,4,128]{2,1,0:T(4,128)S(1)} %bitcast.22), channel_id=1, replica_groups={{0,8,16,24,32,40,48,56,2,10,18,26,34,42,50,58,4,12,20,28,36,44,52,60,6,..., dimensions={0} | all-to-all | bytes 131072 | tf_op jit(solution)/shard_map/all_to_all | solution.py:218
  101.0 1.4 %shard_map.42 = f32[1,4096]{1,0:T(1,128)} custom-call(s32[1,4096]{1,0:T(1,128)S(1)} %get-tuple-element.15.place_ref, f32[4,8,4,128]{3,2,1,0:T(4,128)S(1)} %bitcast.17), custom_call_target="tpu_custom_call" | custom-call | bytes 1048576 | tf_op jit(solution)/shard_map/pallas_call | solution.py:205
  (8 shorter events, 0.1 us)
Async XLA Ops:
  0.0 2.8 %copy-start = (bf16[4096,768]{1,0:T(8,128)(2,1)S(1)}, bf16[4096,768]{1,0:T(8,128)(2,1)}, u32[]{:S(2)}) copy-start(bf16[4096,768]{1,0:T(8,128)(2,1)} %emb_ref.1) | copy-start | bytes 18874372
  48.3 13.3 %collective-permute-start = (bf16[512,768]{1,0:T(8,128)(2,1)S(1)}, bf16[512,768]{1,0:T(8,128)(2,1)S(1)}, u32[]{:S(2)}, u32[]{:S(2)}) collective-permute-start(bf16[512,768]{1,0:T(8,128)(2,1)S(1)} %slice.24.a_ref), channel_id=1, source_target_pairs={{0,2},{2,4},{4,6},{6,0},{1,7},{3,1},{5,3},{7,5},{8,10},{10,12},{12... | collective-permute-start | bytes 2359304 | tf_op jit(solution)/shard_map/ppermute | solution.py:245
  52.9 17.4 %collective-permute-start.1 = (bf16[512,768]{1,0:T(8,128)(2,1)S(1)}, bf16[512,768]{1,0:T(8,128)(2,1)S(1)}, u32[]{:S(2)}, u32[]{:S(2)}) collective-permute-start(bf16[512,768]{1,0:T(8,128)(2,1)S(1)} %slice.24.a_ref), channel_id=1, source_target_pairs={{0,1},{1,0},{2,3},{3,2},{4,5},{5,4},{6,7},{7,6},{8,9},{9,8},{10,11... | collective-permute-start | bytes 2359304 | tf_op jit(solution)/shard_map/ppermute | solution.py:246
  58.2 16.0 %collective-permute-start.3 = (bf16[512,768]{1,0:T(8,128)(2,1)S(1)}, bf16[512,768]{1,0:T(8,128)(2,1)S(1)}, u32[]{:S(2)}, u32[]{:S(2)}) collective-permute-start(bf16[512,768]{1,0:T(8,128)(2,1)S(1)} %slice.24.a_ref), channel_id=1, source_target_pairs={{0,6},{2,0},{4,2},{6,4},{1,3},{3,5},{5,7},{7,1},{8,14},{10,8},{12,... | collective-permute-start | bytes 2359304 | tf_op jit(solution)/shard_map/ppermute | solution.py:253
  61.6 12.5 %collective-permute-start.2 = (bf16[512,768]{1,0:T(8,128)(2,1)S(1)}, bf16[512,768]{1,0:T(8,128)(2,1)S(1)}, u32[]{:S(2)}, u32[]{:S(2)}) collective-permute-start(bf16[512,768]{1,0:T(8,128)(2,1)S(1)} %collective-permute-done.f_ref), channel_id=1, source_target_pairs={{0,1},{1,0},{2,3},{3,2},{4,5},{5,4},{6,7},{7,6},{8,9},{9,8},{10,11... | collective-permute-start | bytes 2359304 | tf_op jit(solution)/shard_map/ppermute | solution.py:254

commit v7 on v6

--- a/solution.py
+++ b/solution.py
@@ -124,10 +124,12 @@
 
 def last_kernel(groups_ref, rows_ref, columns_ref, best_ref, a_ref, b_ref, f_ref, q_ref, s_ref, out_ref):
     f, q, s = f_ref[...], q_ref[...], s_ref[...]
-    b_s = masked_scores(rows_ref, columns_ref, b_ref[...], 1, s, 3)
-    f_s = masked_scores(rows_ref, columns_ref, f, 2, s, 3)
-    a_q = masked_scores(rows_ref, columns_ref, a_ref[...], 0, q, 4)
-    f_q = masked_scores(rows_ref, columns_ref, f, 2, q, 4)
+    with_s = nt_dot(jnp.concatenate([b_ref[...], f], axis=0), s)
+    with_q = nt_dot(jnp.concatenate([a_ref[...], f], axis=0), q)
+    b_s = jnp.where(same_cluster(rows_ref, 1, columns_ref, 3), with_s[:ROWS], -1.0)
+    f_s = jnp.where(same_cluster(rows_ref, 2, columns_ref, 3), with_s[ROWS:], -1.0)
+    a_q = jnp.where(same_cluster(rows_ref, 0, columns_ref, 4), with_q[:ROWS], -1.0)
+    f_q = jnp.where(same_cluster(rows_ref, 2, columns_ref, 4), with_q[ROWS:], -1.0)
     best = spread(
         (row_best(a_q), groups_ref[0]),
         (row_best(b_s), groups_ref[1]),

time: 103 us -> 103 us (level)
  no operation moved by 1% of the time
where the time goes in v7:
time: 103 us; the launch traced here: 102 us
  blocking collectives  66 us (64%)
  starting transfers between devices  20 us (19%)
  Pallas kernels  12 us (12%)
  waiting for transfers between devices  2.51 us (2%)
    all_to_all x1, blocking collectives, on_device(): lax.all_to_all(packed, 'dp', split_axis=0, concat_axis=0, tiled=True)  41.9 us
    all_to_all x2, blocking collectives, exchange(): lax.all_to_all(array, ('dp', 'tile'), split_axis=0, concat_axis=0, axis_i...  24.1 us
    ppermute x1, starting transfers between devices, on_device(): crossed = lax.ppermute(first, 'tile', swap)  8.61 us
    pallas_call x3, Pallas kernels, scores(): return call(kernel, out_shape, specs, flops)(groups, *arrays)  5.7 us
    ppermute x1, starting transfers between devices, on_device(): first = lax.ppermute(a, 'tile', up[0] + down[1])  4.39 us
    ppermute x1, starting transfers between devices, on_device(): b = lax.ppermute(a, 'tile', swap)  3.88 us
    pallas_call x1, Pallas kernels, pack(): call(pack_kernel, jax.ShapeDtypeStruct((ROWS, features + 128), jnp.bfloat...  3.51 us
    ppermute x1, starting transfers between devices, on_device(): second = lax.ppermute(later, 'tile', down[0] + up[1])  3.12 us
  transfers between devices with their start and end apart: 4, of which 2 were waited for; matrix products, arithmetic and copies ran while one was open for 0% of the time, Pallas kernels for 3%

profile of v7, /device:TPU:1, one launch (start us, length us, event | category | flops | bytes accessed | tf_op | source)
XLA Modules:
  0.0 102.4 jit_solution(5966271550238668537)
XLA Ops:
  0.0 0.0 copy-start
  0.0 0.9 compare_select_fusion
  0.9 1.4 %shard_map.37 = (s32[1,4096]{1,0:T(1,128)S(1)}, s32[1,4096]{1,0:T(1,128)S(1)}, bf16[512,128]{1,0:T(8,128)(2,1)S(1)}) custom-call(s32[1]{0:T(128)} %bitcast.tile_ref, s32[1,4096]{1,0:T(1,128)S(1)} %bitcast.19), custom_call_target="tpu_custom_call" | custom-call | flops 2000000000 | bytes 1048576 | tf_op jit(solution)/shard_map/pallas_call | solution.py:183
  2.3 0.5 copy-done
  2.8 3.5 %shard_map.38 = bf16[512,896]{1,0:T(8,128)(2,1)S(1)} custom-call(s32[1,4096]{1,0:T(1,128)S(1)} %get-tuple-element.16.wanted_ref, bf16[512,128]{1,0:T(8,128)(2,1)S(1)} %get-tuple-element.17.tag_ref, bf16[4096,768]{1,0:T(8,128)(2,1)S(1)} %copy-done), custom_call_target="tpu_custom_call" | custom-call | flops 3221225472 | bytes 1048576 | tf_op jit(solution)/shard_map/pallas_call | solution.py:190
  6.3 41.9 %all_to_all.15 = bf16[64,8,896]{2,1,0:T(8,128)(2,1)S(1)} all-to-all(bf16[64,8,896]{2,1,0:T(8,128)(2,1)S(1)} %bitcast.16), channel_id=1, replica_groups=mesh['dp'=64,'tile'=8] {'dp'}, dimensions={0} | all-to-all | bytes 1835008 | tf_op jit(solution)/shard_map/all_to_all | solution.py:241
  48.3 0.1 slice.24.a_ref
  48.3 4.4 %collective-permute-start = (bf16[512,768]{1,0:T(8,128)(2,1)S(1)}, bf16[512,768]{1,0:T(8,128)(2,1)S(1)}, u32[]{:S(2)}, u32[]{:S(2)}) collective-permute-start(bf16[512,768]{1,0:T(8,128)(2,1)S(1)} %slice.24.a_ref), channel_id=1, source_target_pairs={{0,2},{2,4},{4,6},{6,0},{1,7},{3,1},{5,3},{7,5},{8,10},{10,12},{12... | collective-permute-start | bytes 2359304 | tf_op jit(solution)/shard_map/ppermute | solution.py:247
  52.8 0.1 stack.20.groups_ref
  52.9 3.9 %collective-permute-start.1 = (bf16[512,768]{1,0:T(8,128)(2,1)S(1)}, bf16[512,768]{1,0:T(8,128)(2,1)S(1)}, u32[]{:S(2)}, u32[]{:S(2)}) collective-permute-start(bf16[512,768]{1,0:T(8,128)(2,1)S(1)} %slice.24.a_ref), channel_id=1, source_target_pairs={{0,1},{1,0},{2,3},{3,2},{4,5},{5,4},{6,7},{7,6},{8,9},{9,8},{10,11... | collective-permute-start | bytes 2359304 | tf_op jit(solution)/shard_map/ppermute | solution.py:248
  56.8 1.4 %shard_map.39 = (f32[32,128]{1,0:T(8,128)S(1)}, f32[2560,128]{1,0:T(8,128)S(1)}, f32[40,512]{1,0:T(8,128)S(1)}) custom-call(s32[5]{0:T(128)S(1)} %stack.20.groups_ref, bf16[512,128]{1,0:T(8,128)(2,1)S(1)} %slice.25.tag_ref, bf16[512,768]{1,0:T(8,128)(2,1)S(1)} %slice.24.a_ref), custom_call_target="tpu_custom_call" | custom-call | flops 805306368 | bytes 1048576 | tf_op jit(solution)/shard_map/pallas_call | solution.py:202
  58.2 3.1 %collective-permute-start.3 = (bf16[512,768]{1,0:T(8,128)(2,1)S(1)}, bf16[512,768]{1,0:T(8,128)(2,1)S(1)}, u32[]{:S(2)}, u32[]{:S(2)}) collective-permute-start(bf16[512,768]{1,0:T(8,128)(2,1)S(1)} %slice.24.a_ref), channel_id=1, source_target_pairs={{0,6},{2,0},{4,2},{6,4},{1,3},{3,5},{5,7},{7,1},{8,14},{10,8},{12,... | collective-permute-start | bytes 2359304 | tf_op jit(solution)/shard_map/ppermute | solution.py:255
  61.3 0.4 collective-permute-done.f_ref
  61.6 8.6 %collective-permute-start.2 = (bf16[512,768]{1,0:T(8,128)(2,1)S(1)}, bf16[512,768]{1,0:T(8,128)(2,1)S(1)}, u32[]{:S(2)}, u32[]{:S(2)}) collective-permute-start(bf16[512,768]{1,0:T(8,128)(2,1)S(1)} %collective-permute-done.f_ref), channel_id=1, source_target_pairs={{0,1},{1,0},{2,3},{3,2},{4,5},{5,4},{6,7},{7,6},{8,9},{9,8},{10,11... | collective-permute-start | bytes 2359304 | tf_op jit(solution)/shard_map/ppermute | solution.py:256
  70.3 0.0 collective-permute-done.1.b_ref
  70.3 1.7 %shard_map.40.best_ref = f32[32,128]{1,0:T(8,128)S(1)} custom-call(s32[5]{0:T(128)S(1)} %stack.20.groups_ref, f32[2560,128]{1,0:T(8,128)S(1)} %get-tuple-element.20.rows_ref, f32[40,512]{1,0:T(8,128)S(1)} %get-tuple-element.21.columns_ref, f32[32,128]{1,0:T(8,128)S(1)} %get-tuple-element.23.best_ref, bf16[512,768]{1,0:T(8,128)(2,1)S(1)} %slice.24.a_ref, ...), custom_call_target="tpu_custom_call" | custom-call | flops 805306368 | bytes 1048576 | tf_op jit(solution)/shard_map/pallas_call | solution.py:202
  72.0 2.1 %collective-permute-done.3.s_ref = bf16[512,768]{1,0:T(8,128)(2,1)S(1)} collective-permute-done((bf16[512,768]{1,0:T(8,128)(2,1)S(1)}, bf16[512,768]{1,0:T(8,128)(2,1)S(1)}, u32[]{:S(2)}, u32[]{:S(2)}) %collective-permute-start.3) | collective-permute-done | bytes 786464 | tf_op jit(solution)/shard_map/ppermute | solution.py:255
  74.1 0.0 collective-permute-done.2.q_ref
  74.1 2.6 %shard_map.41 = f32[32,128]{1,0:T(8,128)S(1)} custom-call(s32[5]{0:T(128)S(1)} %stack.20.groups_ref, f32[2560,128]{1,0:T(8,128)S(1)} %get-tuple-element.20.rows_ref, f32[40,512]{1,0:T(8,128)S(1)} %get-tuple-element.21.columns_ref, f32[32,128]{1,0:T(8,128)S(1)} %shard_map.40.best_ref, bf16[512,768]{1,0:T(8,128)(2,1)S(1)} %slice.24.a_ref, ...), custom_call_target="tpu_custom_call" | custom-call | flops 805306368 | bytes 1048576 | tf_op jit(solution)/shard_map/pallas_call | solution.py:202
  76.7 11.3 %all_to_all.16 = f32[16,4,128]{2,1,0:T(4,128)S(1)} all-to-all(f32[16,4,128]{2,1,0:T(4,128)S(1)} %bitcast.24), channel_id=1, replica_groups={{0,64,128,192,256,320,384,448,1,65,129,193,257,321,385,449},{2,66,130,1..., dimensions={0} | all-to-all | bytes 65536 | tf_op jit(solution)/shard_map/all_to_all | solution.py:220
  88.1 0.1 fusion.1
  88.2 0.1 pad_maximum_fusion
  88.3 12.7 %all_to_all.17 = f32[32,4,128]{2,1,0:T(4,128)S(1)} all-to-all(f32[32,4,128]{2,1,0:T(4,128)S(1)} %bitcast.22), channel_id=1, replica_groups={{0,8,16,24,32,40,48,56,2,10,18,26,34,42,50,58,4,12,20,28,36,44,52,60,6,..., dimensions={0} | all-to-all | bytes 131072 | tf_op jit(solution)/shard_map/all_to_all | solution.py:220
  101.1 1.4 %shard_map.42 = f32[1,4096]{1,0:T(1,128)} custom-call(s32[1,4096]{1,0:T(1,128)S(1)} %get-tuple-element.15.place_ref, f32[4,8,4,128]{3,2,1,0:T(4,128)S(1)} %bitcast.17), custom_call_target="tpu_custom_call" | custom-call | bytes 1048576 | tf_op jit(solution)/shard_map/pallas_call | solution.py:207
  (8 shorter events, 0.1 us)
Async XLA Ops:
  0.0 2.8 %copy-start = (bf16[4096,768]{1,0:T(8,128)(2,1)S(1)}, bf16[4096,768]{1,0:T(8,128)(2,1)}, u32[]{:S(2)}) copy-start(bf16[4096,768]{1,0:T(8,128)(2,1)} %emb_ref.1) | copy-start | bytes 18874372
  48.3 13.3 %collective-permute-start = (bf16[512,768]{1,0:T(8,128)(2,1)S(1)}, bf16[512,768]{1,0:T(8,128)(2,1)S(1)}, u32[]{:S(2)}, u32[]{:S(2)}) collective-permute-start(bf16[512,768]{1,0:T(8,128)(2,1)S(1)} %slice.24.a_ref), channel_id=1, source_target_pairs={{0,2},{2,4},{4,6},{6,0},{1,7},{3,1},{5,3},{7,5},{8,10},{10,12},{12... | collective-permute-start | bytes 2359304 | tf_op jit(solution)/shard_map/ppermute | solution.py:247
  52.9 17.4 %collective-permute-start.1 = (bf16[512,768]{1,0:T(8,128)(2,1)S(1)}, bf16[512,768]{1,0:T(8,128)(2,1)S(1)}, u32[]{:S(2)}, u32[]{:S(2)}) collective-permute-start(bf16[512,768]{1,0:T(8,128)(2,1)S(1)} %slice.24.a_ref), channel_id=1, source_target_pairs={{0,1},{1,0},{2,3},{3,2},{4,5},{5,4},{6,7},{7,6},{8,9},{9,8},{10,11... | collective-permute-start | bytes 2359304 | tf_op jit(solution)/shard_map/ppermute | solution.py:248
  58.2 16.0 %collective-permute-start.3 = (bf16[512,768]{1,0:T(8,128)(2,1)S(1)}, bf16[512,768]{1,0:T(8,128)(2,1)S(1)}, u32[]{:S(2)}, u32[]{:S(2)}) collective-permute-start(bf16[512,768]{1,0:T(8,128)(2,1)S(1)} %slice.24.a_ref), channel_id=1, source_target_pairs={{0,6},{2,0},{4,2},{6,4},{1,3},{3,5},{5,7},{7,1},{8,14},{10,8},{12,... | collective-permute-start | bytes 2359304 | tf_op jit(solution)/shard_map/ppermute | solution.py:255
  61.6 12.5 %collective-permute-start.2 = (bf16[512,768]{1,0:T(8,128)(2,1)S(1)}, bf16[512,768]{1,0:T(8,128)(2,1)S(1)}, u32[]{:S(2)}, u32[]{:S(2)}) collective-permute-start(bf16[512,768]{1,0:T(8,128)(2,1)S(1)} %collective-permute-done.f_ref), channel_id=1, source_target_pairs={{0,1},{1,0},{2,3},{3,2},{4,5},{5,4},{6,7},{7,6},{8,9},{9,8},{10,11... | collective-permute-start | bytes 2359304 | tf_op jit(solution)/shard_map/ppermute | solution.py:256
